TPU v7x, 256 devices: a whole 4x4x8 slice. The times are simulated.
256 devices in a mesh: src: 8 (over x, y_hi), snk: 8 (over z), mom: 4 (over y_lo, core).
Axes of the slice: x: 4, y: 4 (y_hi: 2, y_lo: 2; y = y_hi * 2 + y_lo), z: 8, core: 2. Of those that a mesh axis runs over, the one named last changes fastest.
Arguments:
- peram_blocks: bfloat16 [32, 8, 2, 512, 512], P('src', 'snk'), may hold values from -5 to 5
- projections: bfloat16 [32, 4, 4, 2, 128, 128], P('src', 'mom'), may hold values from -0.5 to 0.5
- gamma_index: int32 [4, 4], replicated, may hold values from 0 to 15
- partner: int32 [4], P('mom'), may hold values from 0 to 3, each once
- separations: int32 [4], replicated, may hold values from 1 to 31, as said below
Outputs:
- correlator: float32 [32, 4, 4, 2], P(None, None, 'mom')
Inputs may be any that keep to these rules, and one draw needn't show every extreme that they name: Each operator appears once as the partner of a source operator. separations count source time slices; sink slices are taken modulo 32.
All inputs are finite; a program needn't handle non-finite values.
Results may differ from a plain program's by a relative error of at most 0.007.
Values may be sent and summed in bfloat16 or wider, within the bound.
A program may use at most 64 MiB of HBM per device.

v0:
```python
import jax
import jax.numpy as jnp
import numpy as np
from jax import lax
from jax.sharding import PartitionSpec as P

NSEP = 4


def dirac_table():
    zero_matrix = np.zeros((4, 4))
    unit_real = np.eye(4)
    gamma_one = (
        zero_matrix,
        np.array([[0, 0, 0, 1], [0, 0, 1, 0], [0, -1, 0, 0], [-1, 0, 0, 0]], dtype=np.float32),
    )
    gamma_two = (
        np.array([[0, 0, 0, -1], [0, 0, 1, 0], [0, 1, 0, 0], [-1, 0, 0, 0]], dtype=np.float32),
        zero_matrix,
    )
    gamma_three = (
        zero_matrix,
        np.array([[0, 0, 1, 0], [0, 0, 0, -1], [-1, 0, 0, 0], [0, 1, 0, 0]], dtype=np.float32),
    )
    gamma_four = (
        np.array([[0, 0, 1, 0], [0, 0, 0, 1], [1, 0, 0, 0], [0, 1, 0, 0]], dtype=np.float32),
        zero_matrix,
    )
    factors = (gamma_one, gamma_two, gamma_three, gamma_four)
    real_list = []
    imag_list = []
    for gamma_code in range(16):
        real_now = unit_real
        imag_now = zero_matrix
        for position in range(4):
            if gamma_code >> position & 1:
                factor_real, factor_imag = factors[position]
                next_real = real_now @ factor_real - imag_now @ factor_imag
                next_imag = real_now @ factor_imag + imag_now @ factor_real
                real_now = next_real
                imag_now = next_imag
        real_list.append(real_now)
        imag_list.append(imag_now)
    return np.stack([np.stack(real_list), np.stack(imag_list)], axis=1).astype(np.float32)


def build_elementals(projections, gamma_index):
    codes = jnp.arange(16, dtype=jnp.int32)
    one_hot = (gamma_index[:, :, None] == codes[None, None, :]).astype(jnp.float32)
    spin_part = jnp.einsum(
        "prg,gcst->prcst", one_hot, jnp.asarray(dirac_table()).astype(jnp.float32)
    )
    proj_real = projections[:, :, :, 0].astype(jnp.float32)
    proj_imag = projections[:, :, :, 1].astype(jnp.float32)
    form = "prst,wpref->wpsetf"
    real_part = jnp.einsum(form, spin_part[:, :, 0], proj_real) - jnp.einsum(
        form, spin_part[:, :, 1], proj_imag
    )
    imag_part = jnp.einsum(form, spin_part[:, :, 0], proj_imag) + jnp.einsum(
        form, spin_part[:, :, 1], proj_real
    )
    full_width = 4 * projections.shape[-1]
    shape_out = (projections.shape[0], projections.shape[1], full_width, full_width)
    stacked = jnp.stack([real_part.reshape(shape_out), imag_part.reshape(shape_out)], axis=2)
    return stacked.astype(jnp.bfloat16)


def complex_products(blocks, elementals, form):
    real_part = jnp.einsum(
        form, blocks[:, :, 0], elementals[:, :, 0], preferred_element_type=jnp.float32
    )
    real_part = real_part - jnp.einsum(
        form, blocks[:, :, 1], elementals[:, :, 1], preferred_element_type=jnp.float32
    )
    imag_part = jnp.einsum(
        form, blocks[:, :, 0], elementals[:, :, 1], preferred_element_type=jnp.float32
    )
    imag_part = imag_part + jnp.einsum(
        form, blocks[:, :, 1], elementals[:, :, 0], preferred_element_type=jnp.float32
    )
    return jnp.stack([real_part, imag_part], axis=3).astype(jnp.bfloat16)


def sink_products(blocks, elementals):
    return complex_products(blocks, elementals, "woyc,wpcx->wopxy")


def source_products(blocks, elementals):
    return complex_products(blocks, elementals, "woxc,wpcy->wopxy")


def align_sources(backward_raw, shifts):
    source_count = backward_raw.shape[0]
    columns = []
    for sep_index in range(backward_raw.shape[1]):
        targets = (jnp.arange(source_count, dtype=jnp.int32) + shifts[sep_index]) % source_count
        columns.append(jnp.take(backward_raw[:, sep_index], targets, axis=0))
    return jnp.stack(columns, axis=1)


def pair_traces(forward, backward):
    form = "tkpxy,tkpxy->tkp"
    real_part = jnp.einsum(
        form, forward[:, :, :, 0], backward[:, :, :, 0], preferred_element_type=jnp.float32
    )
    real_part = real_part - jnp.einsum(
        form, forward[:, :, :, 1], backward[:, :, :, 1], preferred_element_type=jnp.float32
    )
    imag_part = jnp.einsum(
        form, forward[:, :, :, 0], backward[:, :, :, 1], preferred_element_type=jnp.float32
    )
    imag_part = imag_part + jnp.einsum(
        form, forward[:, :, :, 1], backward[:, :, :, 0], preferred_element_type=jnp.float32
    )
    return jnp.stack([real_part, imag_part], axis=-1)


def shards(peram_blocks, projections, gamma_index, partner, separations):
    src_count = lax.axis_size("src")
    snk_count = lax.axis_size("snk")
    slices_dev = peram_blocks.shape[0]
    offsets_dev = peram_blocks.shape[1]
    full_width = peram_blocks.shape[-1]
    ops_dev = projections.shape[1]
    time_count = slices_dev * src_count
    is_back = lax.axis_index("snk") * offsets_dev >= NSEP
    own_gamma = lax.dynamic_slice_in_dim(gamma_index, lax.axis_index("mom") * ops_dev, ops_dev, 0)
    arrived = lax.all_gather(projections, "mom", axis=1, tiled=True)
    codes = jnp.arange(arrived.shape[1], dtype=jnp.int32)
    selector = (partner[:, None] == codes[None, :]).astype(jnp.bfloat16)
    partner_proj = jnp.einsum(
        "pq,wqrcef->wprcef", selector, arrived, preferred_element_type=jnp.float32
    ).astype(jnp.bfloat16)
    all_codes = jnp.arange(gamma_index.shape[0], dtype=jnp.int32)
    matches = (partner[:, None] == all_codes[None, :]).astype(jnp.int32)
    partner_gamma = jnp.sum(matches[:, :, None] * gamma_index[None, :, :], axis=1)
    chosen_proj = jnp.where(is_back, partner_proj, projections)
    chosen_gamma = jnp.where(is_back, partner_gamma, own_gamma)
    elementals = build_elementals(chosen_proj, chosen_gamma)
    own_products = lax.cond(is_back, sink_products, source_products, peram_blocks, elementals)
    grid_count = src_count * snk_count
    rows_dev = full_width // grid_count
    shaped = own_products.reshape(
        slices_dev, offsets_dev, ops_dev, 2, grid_count, rows_dev, full_width
    )
    received = lax.all_to_all(shaped, ("src", "snk"), split_axis=4, concat_axis=0, tiled=True)
    received = received.reshape(
        src_count, snk_count, slices_dev, offsets_dev, ops_dev, 2, rows_dev, full_width
    )

    def offset_column(offset):
        picked = received[:, offset // offsets_dev, :, offset % offsets_dev]
        return picked.reshape(time_count, ops_dev, 2, rows_dev, full_width)

    forward = jnp.stack([offset_column(sep_index) for sep_index in range(NSEP)], axis=1)
    backward_raw = jnp.stack([offset_column(NSEP + sep_index) for sep_index in range(NSEP)], axis=1)
    backward = align_sources(backward_raw, separations)
    traces = pair_traces(forward, backward)
    return lax.psum(traces * (1.0 / full_width), ("src", "snk"))


def solution(mesh):
    placed = (
        P("src", "snk", None, None, None),
        P("src", "mom", None, None, None, None),
        P(),
        P("mom"),
        P(),
    )
    return jax.shard_map(
        shards, mesh=mesh, in_specs=placed, out_specs=P(None, None, "mom", None), check_vma=False
    )
```

profile of v0, /device:TPU:8, one launch (start us, length us, event | category | flops | bytes accessed | tf_op | source)
XLA Modules:
  0.0 433.7 jit_solution(5409881570065282172)
XLA Ops:
  10.6 48.9 %all-gather.2.cloned.1.call-done = bf16[4,4,4,2,128,128]{5,4,3,2,1,0:T(8,128)(2,1)} async-done(((bf16[4,1,4,2,128,128]{5,4,3,2,1,0:T(8,128)(2,1)}), bf16[4,4,4,2,128,128]{5,4,3,2,1,0:T(8,128)(2,1)}) %all-gather.2.cloned.1.call-update) | async-done | bytes 4194320 | tf_op jit(solution)/shard_map/all_gather | solution.py:128
  59.5 5.6 %fusion.4 = bf16[1,4,4,2,128,128]{5,0,4,3,2,1:T(2,128)(2,1)S(1)} fusion(bf16[4,4,4,2,128,128]{5,4,3,2,1,0:T(8,128)(2,1)} %all-gather.2.cloned.1.call-done, s32[]{:T(128)} %bitcast.199), kind=kOutput, calls=%fused_computation.26 | convolution fusion | flops 4194308 | bytes 5242884 | tf_op jit(solution)/shard_map/pq,wqrcef->wprcef/dot_general | solution.py:131
  65.1 1.9 fusion.13
  68.2 3.2 fusion.19
  73.6 2.4 stack.52
  76.0 3.4 fusion.11
  80.4 2.3 stack.53
  82.7 4.5 %pad_maximum_fusion.2 = bf16[4,1,2,512,512]{4,3,0,2,1:T(8,128)(2,1)} fusion(bf16[4,1,1,512,512]{4,3,0,2,1:T(8,128)(2,1)} %stack.53, bf16[4,1,1,512,512]{4,3,0,2,1:T(8,128)(2,1)} %stack.52), kind=kLoop, calls=%fused_computation.22 | loop fusion | flops 2097152 | bytes 8388608 | tf_op jit(solution)/shard_map/stack | solution.py:64
  87.2 18.2 %conditional.2 = (bf16[4,1,1,2,512,512]{4,5,0,3,2,1:T(8,128)(2,1)}) conditional(s32[]{:T(128)} %convert_element_type.40, (bf16[4,1,2,512,512]{4,3,0,2,1:T(8,128)(2,1)}, bf16[4,1,2,512,512]{4,3,2,1,0:T(8,128)(2,1)}) %tuple.15, (bf16[4,1,2,512,512]{4,3,0,2,1:T(8,128)(2,1)}, bf16[4,1,2,512,512]{4,3,2,1,0:T(8,128)(2,1)}) %tuple.15), branch_computations={%region_1.2_spmd, %region_2.3_spmd} | conditional | flops 4301258752 | bytes 96469056
  87.2 7.3 %copy.65 = bf16[4,1,2,512,512]{3,4,0,2,1:T(8,128)(2,1)} copy(bf16[4,1,2,512,512]{4,3,0,2,1:T(8,128)(2,1)} %get-tuple-element.35) | data formatting | bytes 8388608 | tf_op jit(solution)/shard_map
  94.6 3.7 fusion
  99.3 1.3 subtract_bitcast_fusion
  100.6 1.3 fusion.1
  101.9 1.3 add_bitcast_fusion
  103.2 2.3 pad_maximum_fusion
  105.5 7.3 %copy.69 = bf16[4,1,1,2,512,512]{5,4,3,0,2,1:T(8,128)(2,1)} copy(bf16[4,1,1,2,512,512]{4,5,0,3,2,1:T(8,128)(2,1)} %get-tuple-element.61) | data formatting | bytes 8388608 | tf_op jit(solution)/shard_map/conditional
  112.7 4.8 %copy.70 = bf16[4,1,1,2,64,8,512]{6,5,3,0,2,1,4:T(8,128)(2,1)} copy(bf16[4,1,1,2,64,8,512]{6,5,4,3,0,2,1:T(8,128)(2,1)} %bitcast.201) | data formatting | bytes 8388608 | tf_op jit(solution)/shard_map/reshape | solution.py:143
  117.6 20.2 %all-to-all-start = ((bf16[4,1,1,2,64,8,512]{6,5,3,0,2,1,4:T(8,128)(2,1)}), bf16[4,1,1,2,64,8,512]{6,5,3,0,2,1,4:T(8,128)(2,1)}, u32[]{:S(2)}, u32[]{:S(2)}) async-start(bf16[4,1,1,2,64,8,512]{6,5,3,0,2,1,4:T(8,128)(2,1)} %copy.70), calls=%async_computation | async-start | bytes 8388608 | tf_op jit(solution)/shard_map/all_to_all | solution.py:146
  143.6 93.4 %all-to-all-done = bf16[4,1,1,2,64,8,512]{6,5,3,0,2,1,4:T(8,128)(2,1)} async-done(((bf16[4,1,1,2,64,8,512]{6,5,3,0,2,1,4:T(8,128)(2,1)}), bf16[4,1,1,2,64,8,512]{6,5,3,0,2,1,4:T(8,128)(2,1)}, u32[]{:S(2)}, u32[]{:S(2)}) %all-to-all-start) | async-done | bytes 4194336 | tf_op jit(solution)/shard_map/all_to_all | solution.py:146
  237.0 3.7 fusion.33
  240.7 1.4 gather_fusion
  243.9 1.3 fusion.16
  245.9 2.2 fusion.8
  248.2 178.1 %psum.7 = f32[32,4,1,2]{0,1,3,2:T(4,128)S(1)} all-reduce(f32[32,4,1,2]{0,1,3,2:T(4,128)S(1)} %maximum_multiply_fusion), channel_id=1, replica_groups=mesh['src'=8,'snk'=8,'mom'=4] {'src','snk'}, use_global_device_ids=true, to_apply=%region_3.5 | all-reduce | flops 256 | bytes 2048 | tf_op jit(solution)/shard_map/psum | solution.py:159
  (49 shorter events, 17.7 us)
Async XLA Ops:
  6.5 52.9 %all-gather.2.cloned.1.call-start = ((), (), s32[]{:S(2)}) async-start(), calls=%async_computation.1 | async-start | bytes 5242880 | tf_op jit(solution)/shard_map/all_gather | solution.py:128
  59.5 5.6 %copy-start.4 = (bf16[4,1,4,2,128,128]{5,4,3,2,1,0:T(8,128)(2,1)S(1)}, bf16[4,1,4,2,128,128]{5,4,3,2,1,0:T(8,128)(2,1)}, u32[]{:S(2)}) copy-start(bf16[4,1,4,2,128,128]{5,4,3,2,1,0:T(8,128)(2,1)} %param.11) | copy-start | bytes 3145732
  94.6 3.7 copy-start
  94.6 4.7 %copy-start.2 = (bf16[4,1,2,512,512]{3,4,0,2,1:T(8,128)(2,1)S(1)}, bf16[4,1,2,512,512]{3,4,0,2,1:T(8,128)(2,1)}, u32[]{:S(2)}) copy-start(bf16[4,1,2,512,512]{3,4,0,2,1:T(8,128)(2,1)} %copy.65) | copy-start | bytes 12582916 | tf_op jit(solution)/shard_map/conditional
  117.5 20.2 %copy-start.7 = (s32[4]{0:T(128)S(1)}, s32[4]{0:T(128)}, u32[]{:S(2)}) copy-start(s32[4]{0:T(128)} %param.14) | copy-start | bytes 52
  117.6 119.5 %all-to-all-start = ((bf16[4,1,1,2,64,8,512]{6,5,3,0,2,1,4:T(8,128)(2,1)}), bf16[4,1,1,2,64,8,512]{6,5,3,0,2,1,4:T(8,128)(2,1)}, u32[]{:S(2)}, u32[]{:S(2)}) async-start(bf16[4,1,1,2,64,8,512]{6,5,3,0,2,1,4:T(8,128)(2,1)} %copy.70), calls=%async_computation | async-start | bytes 8388608 | tf_op jit(solution)/shard_map/all_to_all | solution.py:146
  243.8 1.8 copy-start.5
  243.8 1.8 copy-start.6
Sparse Core Ops, SparseCore 0:
  9.2 50.2 all-gather.1
where the time goes:
time: 435 us; the launch traced here: 434 us
  blocking collectives  178 us (41%)
  waiting for transfers between devices  143 us (33%)
  local copies, waits for them, and re-layouts  35.5 us (8%)
  matrix products  23 us (5%)
  starting transfers between devices  20.2 us (5%)
  other arithmetic  19.5 us (4%)
  between operations  14.3 us (3%)
    psum x1, blocking collectives, shards(): return lax.psum(traces * (1.0 / full_width), ('src', 'snk'))  178 us
    all_to_all x1, waiting for transfers between devices, shards(): lax.all_to_all(shaped, ('src', 'snk'), split_axis=4, concat_axis=0, tiled...  93.4 us
    all_gather x1, waiting for transfers between devices, shards(): arrived = lax.all_gather(projections, 'mom', axis=1, tiled=True)  48.9 us
    all_to_all x1, starting transfers between devices, shards(): lax.all_to_all(shaped, ('src', 'snk'), split_axis=4, concat_axis=0, tiled...  20.2 us
    another operation x9, local copies, waits for them, and re-layouts  15.9 us
  transfers between devices with their start and end apart: 2, of which 2 were waited for; matrix products, arithmetic and copies ran while one was open for 2% of the time, Pallas kernels for 0%

commit v1 on v0

v1 whole, which is shorter than its diff:
```python
import functools

import jax
import jax.numpy as jnp
import numpy as np
from jax import lax
from jax.experimental import pallas as pl
from jax.experimental.pallas import tpu as pltpu
from jax.sharding import PartitionSpec as P

MESH = pl.DeviceIdType.MESH
NSEP = 4
ROLE_B_PLANES = (6, 3, 0, 5)


def gamma_table():
    unit = np.eye(4, dtype=complex)
    one = np.array([[0, 0, 0, 1j], [0, 0, 1j, 0], [0, -1j, 0, 0], [-1j, 0, 0, 0]])
    two = np.array([[0, 0, 0, -1], [0, 0, 1, 0], [0, 1, 0, 0], [-1, 0, 0, 0]], dtype=complex)
    three = np.array([[0, 0, 1j, 0], [0, 0, 0, -1j], [-1j, 0, 0, 0], [0, 1j, 0, 0]])
    four = np.array([[0, 0, 1, 0], [0, 0, 0, 1], [1, 0, 0, 0], [0, 1, 0, 0]], dtype=complex)
    rows = []
    for code in range(16):
        value = unit
        for position, factor in enumerate((one, two, three, four)):
            if code >> position & 1:
                value = value @ factor
        pattern = int(np.flatnonzero(np.abs(value[:, 0]))[0])
        powers = [(1, 1j, -1, -1j).index(complex(value[s ^ pattern, s])) for s in range(4)]
        rows.append([pattern] + powers)
    return np.array(rows, dtype=np.int32).reshape(-1)


def body(
    sep_ref, gam_ref, part_ref, tab_ref, p_ref, e_ref, out_ref,
    e_in, p_in, e_snd, p_snd, pl_snd, el_snd, e1, p1, e2s, p2s, eloc, erem, prem, pn,
    fbuf, nbuf, ptr, partbuf, res, r1, t2, r2, lsem, ssem, rsem,
):
    src, z, mom = lax.axis_index("src"), lax.axis_index("snk"), lax.axis_index("mom")
    c, e = mom // 2, mom % 2
    u = 2 * src + c
    me = 4 * src + mom
    k = (z + 2) % 4
    sep = sep_ref[k]
    odd = sep & 1
    role_a = (z + z // 2 + z // 4) % 2
    is_a = role_a == 1
    shift = jnp.where(is_a, sep >> 1, 16 - ((sep + 1) >> 1))
    par_loc = jnp.where(is_a, 0, (1 + odd) & 1)
    par_rem = jnp.where(is_a, odd, 1)
    odd_own = sep_ref[z % 4] & 1
    snd_rem = jnp.where(z < NSEP, 1, odd_own)
    snd_loc = jnp.where(z < NSEP, 0, (1 + odd_own) & 1)
    z_even = 1 - z % 2
    z_rem = (z + 2 + 4 * z_even) % 8
    z_loc = (z + 6 + 4 * z_even) % 8

    def remote(src_ref, dst_ref, index, target):
        return pltpu.make_async_remote_copy(
            src_ref=src_ref, dst_ref=dst_ref, send_sem=ssem.at[index], recv_sem=rsem.at[index],
            device_id=target, device_id_type=MESH,
        )

    def arrived(ref, index):
        pltpu.make_async_copy(ref, ref, rsem.at[index]).wait()

    def left(ref, index):
        pltpu.make_async_copy(ref, ref, ssem.at[index]).wait()

    other_core = (src, z, 2 * c + 1 - e)
    other_chip = (src, z, 2 * (1 - c) + e)

    load_e = pltpu.make_async_copy(e_ref, e_in, lsem.at[0])
    load_e.start()
    load_p = pltpu.make_async_copy(
        p_ref.at[pl.ds(2 * c, 2), 0, :, pl.ds(pl.multiple_of(256 * e, 256), 256), :], p_in, lsem.at[1]
    )
    load_p.start()
    partbuf[mom] = jnp.full((8, 128), part_ref[0], jnp.int32)

    def send_partner(d, carry):
        remote(partbuf.at[mom], partbuf.at[mom], 0, (src, z, (mom + d) % 4)).start()
        return carry

    lax.fori_loop(1, 4, send_partner, 0)

    load_e.wait()
    for h in range(2):
        e_snd[h] = e_in[2 * h + par_rem]

    def send_e1(d, carry):
        i = (me + d) % 32
        rows = pl.ds(pl.multiple_of(32 * i, 32), 32)
        remote(e_snd.at[:, rows, :], e1.at[me], 1, (i // 4, z, i % 4)).start()
        return carry

    lax.fori_loop(1, 32, send_e1, 0)
    own_rows = pl.ds(pl.multiple_of(32 * me, 32), 32)
    e1[me] = e_snd[:, own_rows, :]

    load_p.wait()
    p_snd[...] = p_in[snd_rem]

    def send_p1(d, carry):
        j = (u + d) % 16
        rows = pl.ds(pl.multiple_of(16 * j, 16), 16)
        remote(p_snd.at[:, rows, :], p1.at[u], 2, (j // 2, z_rem, 2 * (j % 2) + e)).start()
        return carry

    lax.fori_loop(0, 16, send_p1, 0)

    eloc[mom] = e_in[2 * c + par_loc]
    el_snd[...] = e_in[2 * (1 - c) + par_loc]
    own_e = remote(eloc.at[mom], eloc.at[mom], 3, other_core)
    own_e.start()
    cross_e = remote(el_snd, eloc.at[mom], 4, other_chip)
    cross_e.start()
    half = pl.ds(pl.multiple_of(256 * e, 256), 256)
    other_half = pl.ds(pl.multiple_of(256 * (1 - e), 256), 256)
    for s in range(4):
        pl_snd[:, s] = p_in[snd_loc, :, :, pl.ds(128 * s, 128)]
    direct_p = remote(pl_snd, pn.at[pl.ds(0, 2), :, half, :], 5, (src, z_loc, mom))
    direct_p.start()

    arrived(partbuf.at[pl.ds(0, 3)], 0)
    partners = [partbuf[o, 0, 0] for o in range(4)]
    arrived(e1.at[pl.ds(0, 31)], 1)

    def rem_op(core, a):
        return jnp.where(is_a, jnp.where(core == 0, partners[2 * a], partners[2 * a + 1]), core + 2 * a)

    def pick_e(i, a):
        block = (i // 2 + shift) % 16
        return e1[(block // 2) * 4 + rem_op(i % 2, a), block % 2]

    def send_e2(d, carry):
        i = (me + d) % 32
        for a in range(2):
            e2s[i, a] = pick_e(i, a)
        remote(e2s.at[i], erem.at[:, own_rows, :], 6, (i // 4, z, i % 4)).start()
        return carry

    lax.fori_loop(1, 32, send_e2, 0)
    for a in range(2):
        erem[a, own_rows, :] = pick_e(me, a)

    arrived(p1, 2)
    own_strip = pl.ds(pl.multiple_of(256 * e + 16 * u, 16), 16)

    def send_p2(d, carry):
        j = (u + d) % 16
        p2s[j] = p1[(j + shift) % 16]
        remote(p2s.at[j], prem.at[:, own_strip, :], 7, (j // 2, z, 2 * (j % 2) + e)).start()
        return carry

    lax.fori_loop(1, 16, send_p2, 0)
    prem[:, own_strip, :] = p1[(u + shift) % 16]

    cross_e.wait_recv()
    from_chip = eloc.at[2 * (1 - c) + e]
    pass_e = remote(from_chip, from_chip, 8, other_core)
    pass_e.start()
    direct_p.wait_recv()
    own_part = pn.at[pl.ds(0, 2), :, half, :]
    pass_p = remote(own_part, own_part, 9, other_core)
    pass_p.start()
    own_e.wait_recv()
    pass_e.wait_recv()
    pass_p.wait_recv()

    pn[2] = -pn[0]
    pn[3] = -pn[1]

    def scalars(code):
        return tab_ref[5 * code], [tab_ref[5 * code + 1 + s] for s in range(4)]

    def times_local(step, carry):
        a, s = step // 4, step % 4
        op = jnp.where(is_a, e + 2 * a, partbuf[e + 2 * a, 0, 0])
        left_re, left_im, right = [], [], []
        for r in range(4):
            code = gam_ref[op, r]
            pattern = tab_ref[5 * code]
            power = tab_ref[5 * code + 1 + s]
            left_re.append(pn[(4 - power) % 4, s ^ pattern])
            left_im.append(pn[(5 - power) % 4, s ^ pattern])
            right.append(
                jnp.concatenate([eloc[op, pl.ds(256 * r, 128), :], eloc[op, pl.ds(256 * r + 128, 128), :]], axis=1)
            )
        right = jnp.concatenate(right, axis=0)
        by_re = jnp.dot(jnp.concatenate(left_re, axis=1), right, preferred_element_type=jnp.float32)
        by_im = jnp.dot(jnp.concatenate(left_im, axis=1), right, preferred_element_type=jnp.float32)
        lanes = pl.ds(pl.multiple_of(128 * s, 128), 128)
        fbuf[a, pl.ds(0, 512), lanes] = (by_re[:, :128] - by_im[:, 128:]).astype(jnp.bfloat16)
        fbuf[a, pl.ds(512, 512), lanes] = (by_re[:, 128:] + by_im[:, :128]).astype(jnp.bfloat16)
        return carry

    lax.fori_loop(0, 8, times_local, 0)

    arrived(e1.at[pl.ds(0, 31)], 6)

    def turn(step, carry):
        rows = pl.ds(pl.multiple_of(128 * (step % 8), 128), 128)
        ptr[step] = erem[step // 8, rows, :].astype(jnp.float32).T
        return carry

    lax.fori_loop(0, 16, turn, 0)

    arrived(p1.at[pl.ds(0, 15)], 7)
    own_rem = prem.at[:, half, :]
    pass_r = remote(own_rem, own_rem, 10, other_core)
    pass_r.start()
    pass_r.wait_recv()

    lane = lax.broadcasted_iota(jnp.int32, (8, 128), 1)
    for a in range(2):

        def times_remote(step, carry):
            cols = pl.ds(pl.multiple_of(256 * step, 256), 256)
            by_re = jnp.dot(fbuf[a], prem[0, :, cols], preferred_element_type=jnp.float32)
            by_im = jnp.dot(fbuf[a], prem[1, :, cols], preferred_element_type=jnp.float32)
            n_re = by_re[:512] - by_im[512:]
            n_im = by_re[512:] + by_im[:512]
            for s in range(2):
                nbuf[0, 2 * step + s] = n_re[:, 128 * s : 128 * s + 128]
                nbuf[1, 2 * step + s] = n_im[:, 128 * s : 128 * s + 128]
            return carry

        lax.fori_loop(0, 2, times_remote, 0)
        op = rem_op(e, a)

        def close(r, carry):
            acc_re, acc_im = carry
            code = gam_ref[op, r]
            pattern = tab_ref[5 * code]
            sum_re = jnp.zeros((128, 128), jnp.float32)
            sum_im = jnp.zeros((128, 128), jnp.float32)
            for s in range(4):
                power = tab_ref[5 * code + 1 + s]
                ca = jnp.where(power == 0, 1.0, jnp.where(power == 2, -1.0, 0.0))
                cb = jnp.where(power == 1, 1.0, jnp.where(power == 3, -1.0, 0.0))
                n_re = nbuf[0, s ^ pattern, pl.ds(128 * s, 128), :]
                n_im = nbuf[1, s ^ pattern, pl.ds(128 * s, 128), :]
                sum_re += ca * n_re - cb * n_im
                sum_im += ca * n_im + cb * n_re
            t_re, t_im = ptr[8 * a + 2 * r], ptr[8 * a + 2 * r + 1]
            return acc_re + sum_re * t_re - sum_im * t_im, acc_im + sum_re * t_im + sum_im * t_re

        zero = jnp.zeros((128, 128), jnp.float32)
        acc_re, acc_im = lax.fori_loop(0, 4, close, (zero, zero))
        res[a] = jnp.where(
            lane == 2 * k, jnp.sum(acc_re) / 512, jnp.where(lane == 2 * k + 1, jnp.sum(acc_im) / 512, 0.0)
        )

    def send_r1(d, carry):
        remote(res, r1.at[z], 11, (src, (z + d) % 8, mom)).start()
        return carry

    lax.fori_loop(1, 8, send_r1, 0)
    r1[z] = res[...]
    arrived(r1.at[pl.ds(0, 7)], 11)
    row = lax.broadcasted_iota(jnp.int32, (8, 128), 0)
    for a in range(2):
        tile = jnp.zeros((8, 128), jnp.float32)
        for plane in range(8):
            tile = jnp.where(row == plane, r1[plane, a], tile)
        t2[a] = tile

    def send_r2(d, carry):
        j = (u + d) % 16
        remote(t2.at[j % 2], r2.at[u], 12, (j // 2, z, 2 * (j % 2) + e)).start()
        return carry

    lax.fori_loop(1, 16, send_r2, 0)
    r2[u] = t2[c]
    arrived(r2.at[pl.ds(0, 15)], 12)

    odd_planes = (row == 0) | (row == 3) | (row == 5) | (row == 6)

    def gather(v, carry):
        even_row = jnp.sum(jnp.where(odd_planes, 0.0, r2[v]), axis=0, keepdims=True)
        tile = jnp.zeros((8, 128), jnp.float32)
        for kk in range(NSEP):
            sep_k = sep_ref[kk]
            block = ((2 * v + 1 + sep_k - ((1 + sep_k) & 1)) // 2) % 16
            tile += jnp.where(row == ROLE_B_PLANES[kk], r2[block], 0.0)
        odd_row = jnp.sum(tile, axis=0, keepdims=True)
        out_ref[v] = jnp.concatenate([even_row, odd_row], axis=0)
        return carry

    lax.fori_loop(0, 16, gather, 0)

    left(partbuf.at[pl.ds(0, 3)], 0)
    left(e1.at[pl.ds(0, 31)], 1)
    left(p1, 2)
    own_e.wait_send()
    cross_e.wait_send()
    direct_p.wait_send()
    left(e1.at[pl.ds(0, 31)], 6)
    left(p1.at[pl.ds(0, 15)], 7)
    pass_e.wait_send()
    pass_p.wait_send()
    pass_r.wait_send()
    left(r1.at[pl.ds(0, 7)], 11)
    left(r2.at[pl.ds(0, 15)], 12)


def shards(peram_blocks, projections, gamma_index, partner, separations):
    bf, f32 = jnp.bfloat16, jnp.float32
    smem = pl.BlockSpec(memory_space=pltpu.SMEM)
    anywhere = pl.BlockSpec(memory_space=pl.ANY)
    out = pl.pallas_call(
        body,
        out_shape=jax.ShapeDtypeStruct((16, 2, 128), f32),
        in_specs=[smem] * 4 + [anywhere] * 2,
        out_specs=pl.BlockSpec(memory_space=pltpu.VMEM),
        scratch_shapes=[
            pltpu.VMEM((4, 1024, 128), bf),
            pltpu.VMEM((2, 2, 256, 512), bf),
            pltpu.VMEM((2, 1024, 128), bf),
            pltpu.VMEM((2, 256, 512), bf),
            pltpu.VMEM((2, 4, 256, 128), bf),
            pltpu.VMEM((1024, 128), bf),
            pltpu.VMEM((32, 2, 32, 128), bf),
            pltpu.VMEM((16, 2, 16, 512), bf),
            pltpu.VMEM((32, 2, 32, 128), bf),
            pltpu.VMEM((16, 2, 16, 512), bf),
            pltpu.VMEM((4, 1024, 128), bf),
            pltpu.VMEM((2, 1024, 128), bf),
            pltpu.VMEM((2, 512, 512), bf),
            pltpu.VMEM((4, 4, 512, 128), bf),
            pltpu.VMEM((2, 1024, 512), bf),
            pltpu.VMEM((2, 4, 512, 128), f32),
            pltpu.VMEM((16, 128, 128), f32),
            pltpu.VMEM((4, 8, 128), jnp.int32),
            pltpu.VMEM((2, 8, 128), f32),
            pltpu.VMEM((8, 2, 8, 128), f32),
            pltpu.VMEM((2, 8, 128), f32),
            pltpu.VMEM((16, 8, 128), f32),
            pltpu.SemaphoreType.DMA((2,)),
            pltpu.SemaphoreType.DMA((13,)),
            pltpu.SemaphoreType.DMA((13,)),
        ],
        compiler_params=pltpu.CompilerParams(has_side_effects=True, vmem_limit_bytes=48 * 1024 * 1024),
    )(
        separations,
        gamma_index,
        partner,
        jnp.asarray(gamma_table()),
        peram_blocks,
        projections.reshape(4, 1024, 128),
    )
    return out[:, :, : 2 * NSEP].reshape(32, NSEP, 1, 2)


def solution(mesh):
    placed = (
        P("src", "snk", None, None, None),
        P("src", "mom", None, None, None, None),
        P(),
        P("mom"),
        P(),
    )
    return jax.shard_map(
        shards, mesh=mesh, in_specs=placed, out_specs=P(None, None, "mom", None), check_vma=False
    )
```

time: 435 us -> 76.8 us (0.18)
  the two profiles are of different devices: /device:TPU:8 before, /device:TPU:1 now
where the time goes in v1:
time: 76.8 us; the launch traced here: 76.4 us
  Pallas kernels  69.5 us (90%)
  local copies, waits for them, and re-layouts  6.19 us (8%)
    pallas_call x1, Pallas kernels, shards(): pl.pallas_call(body, out_shape=jax.ShapeDtypeStruct((16, 2, 128), f32), i...  69.5 us
    unnamed x10, local copies, waits for them, and re-layouts  5.4 us

profile of v1, /device:TPU:1, one launch (start us, length us, event | category | flops | bytes accessed | tf_op | source)
XLA Modules:
  0.0 76.4 jit_solution(17843046476076299125)
XLA Ops:
  0.7 0.0 copy-start
  0.7 2.2 %copy-done = bf16[4,1,2,512,512]{4,3,2,1,0:T(8,128)(2,1)S(1)} copy-done((bf16[4,1,2,512,512]{4,3,2,1,0:T(8,128)(2,1)S(1)}, bf16[4,1,2,512,512]{4,3,2,1,0:T(8,128)(2,1)}, u32[]{:S(2)}) %copy-start) | copy-done | bytes 4194328
  2.8 0.0 copy-start.1
  2.8 1.2 %copy-done.1 = bf16[4,1,4,2,128,128]{5,4,3,2,1,0:T(8,128)(2,1)S(1)} copy-done((bf16[4,1,4,2,128,128]{5,4,3,2,1,0:T(8,128)(2,1)S(1)}, bf16[4,1,4,2,128,128]{5,4,3,2,1,0:T(8,128)(2,1)}, u32[]{:S(2)}) %copy-start.1) | copy-done | bytes 1048600
  4.1 0.0 copy-start.2
  4.1 0.7 copy-done.2
  4.7 0.0 copy-start.3
  4.8 0.7 copy-done.3
  5.4 0.0 copy-start.4
  5.4 0.7 copy-done.4
  6.1 69.5 %shard_map.64 = f32[16,2,128]{2,1,0:T(2,128)S(1)} custom-call(s32[4]{0:T(128)S(1)} %copy-done.3, s32[4,4]{1,0:T(4,128)S(1)} %copy-done.2, s32[1]{0:T(128)S(6)} %copy.12.part_ref, s32[80]{0:T(128)S(1)} %copy-done.4, bf16[4,1,2,512,512]{4,3,2,1,0:T(8,128)(2,1)S(1)} %copy-done, bf16[4,1024,128]{2,1,0:T(8,128)(2,1)S(1)} %bitcast.2), custom_call_target="tpu_custom_call" | custom-call | tf_op jit(solution)/shard_map/pallas_call | solution.py:312
  75.6 0.1 reshape.8
  75.7 0.7 copy.9
Async XLA Ops:
  0.7 2.2 %copy-start = (bf16[4,1,2,512,512]{4,3,2,1,0:T(8,128)(2,1)S(1)}, bf16[4,1,2,512,512]{4,3,2,1,0:T(8,128)(2,1)}, u32[]{:S(2)}) copy-start(bf16[4,1,2,512,512]{4,3,2,1,0:T(8,128)(2,1)} %p_ref.1) | copy-start | bytes 12582916
  2.8 1.2 %copy-start.1 = (bf16[4,1,4,2,128,128]{5,4,3,2,1,0:T(8,128)(2,1)S(1)}, bf16[4,1,4,2,128,128]{5,4,3,2,1,0:T(8,128)(2,1)}, u32[]{:S(2)}) copy-start(bf16[4,1,4,2,128,128]{5,4,3,2,1,0:T(8,128)(2,1)} %param.7) | copy-start | bytes 3145732
  4.1 0.7 copy-start.2
  4.7 0.7 copy-start.3
  5.4 0.7 copy-start.4

commit v2 on v1

v2 whole, which is shorter than its diff:
```python
import functools

import jax
import jax.numpy as jnp
import numpy as np
from jax import lax
from jax.experimental import pallas as pl
from jax.experimental.pallas import tpu as pltpu
from jax.sharding import PartitionSpec as P

MESH = pl.DeviceIdType.MESH
NSEP = 4
ROLE_B_PLANES = (6, 3, 0, 5)


def gamma_table():
    unit = np.eye(4, dtype=complex)
    one = np.array([[0, 0, 0, 1j], [0, 0, 1j, 0], [0, -1j, 0, 0], [-1j, 0, 0, 0]])
    two = np.array([[0, 0, 0, -1], [0, 0, 1, 0], [0, 1, 0, 0], [-1, 0, 0, 0]], dtype=complex)
    three = np.array([[0, 0, 1j, 0], [0, 0, 0, -1j], [-1j, 0, 0, 0], [0, 1j, 0, 0]])
    four = np.array([[0, 0, 1, 0], [0, 0, 0, 1], [1, 0, 0, 0], [0, 1, 0, 0]], dtype=complex)
    rows = []
    for code in range(16):
        value = unit
        for position, factor in enumerate((one, two, three, four)):
            if code >> position & 1:
                value = value @ factor
        pattern = int(np.flatnonzero(np.abs(value[:, 0]))[0])
        powers = [(1, 1j, -1, -1j).index(complex(value[s ^ pattern, s])) for s in range(4)]
        rows.append([pattern] + powers)
    return np.array(rows, dtype=np.int32).reshape(-1)


def body(
    sep_hbm, gam_hbm, part_hbm, tab_hbm, p_ref, e_ref, out_ref,
    sep_ref, gam_ref, part_ref, tab_ref,
    e_in, p_in, e_snd, p_snd, pl_snd, el_snd, e1, p1_re, p1_im, e2s, p2s, eloc, erem, prem, pn,
    fbuf, nbuf, ptr, partbuf, res, r1, t2, r2, lsem, ssem, rsem,
):
    src, z, mom = lax.axis_index("src"), lax.axis_index("snk"), lax.axis_index("mom")
    c, e = mom // 2, mom % 2
    u = 2 * src + c
    me = 4 * src + mom
    k = (z + 2) % 4
    z_even = 1 - z % 2
    z_rem = (z + 2 + 4 * z_even) % 8
    z_loc = (z + 6 + 4 * z_even) % 8

    def remote(src_ref, dst_ref, index, target):
        return pltpu.make_async_remote_copy(
            src_ref=src_ref, dst_ref=dst_ref, send_sem=ssem.at[index], recv_sem=rsem.at[index],
            device_id=target, device_id_type=MESH,
        )

    def arrived(ref, index):
        pltpu.make_async_copy(ref, ref, rsem.at[index]).wait()

    def left(ref, index):
        pltpu.make_async_copy(ref, ref, ssem.at[index]).wait()

    p1 = (p1_re, p1_im)
    other_core = (src, z, 2 * c + 1 - e)
    other_chip = (src, z, 2 * (1 - c) + e)
    half = pl.ds(pl.multiple_of(256 * e, 256), 256)
    own_rows = pl.ds(pl.multiple_of(32 * me, 32), 32)
    own_strip = pl.ds(pl.multiple_of(256 * e + 16 * u, 16), 16)

    loads = [
        pltpu.make_async_copy(one, two, lsem.at[index])
        for index, (one, two) in enumerate(
            (
                (part_hbm, part_ref),
                (sep_hbm, sep_ref),
                (gam_hbm, gam_ref),
                (tab_hbm, tab_ref),
                (e_ref, e_in),
                (p_ref.at[pl.ds(2 * c, 2), 0, :, half, :], p_in),
            )
        )
    ]
    for load in loads:
        load.start()

    barrier = pltpu.get_barrier_semaphore()

    def greet(target):
        pl.semaphore_signal(barrier, inc=1, device_id=target, device_id_type=MESH)

    def greet_blocks(d, carry):
        j = (u + d) % 16
        greet((j // 2, z_loc, 2 * (j % 2) + e))
        return carry

    def greet_plane(d, carry):
        i = (me + d) % 32
        greet((i // 4, z, i % 4))
        return carry

    lax.fori_loop(0, 16, greet_blocks, 0)
    greet((src, z_rem, mom))
    for d in (1, 3, 4, 5, 7):
        greet((src, (z + d) % 8, mom))
    lax.fori_loop(1, 32, greet_plane, 0)

    for load in loads[:5]:
        load.wait()
    sep = sep_ref[k]
    odd = sep & 1
    is_a = (z + z // 2 + z // 4) % 2 == 1
    shift = jnp.where(is_a, sep >> 1, 16 - ((sep + 1) >> 1))
    par_loc = jnp.where(is_a, 0, (1 + odd) & 1)
    par_rem = jnp.where(is_a, odd, 1)
    odd_own = sep_ref[z % 4] & 1
    snd_rem = jnp.where(z < NSEP, 1, odd_own)
    snd_loc = jnp.where(z < NSEP, 0, (1 + odd_own) & 1)
    partbuf[mom] = jnp.full((8, 128), part_ref[0], jnp.int32)
    for h in range(2):
        e_snd[h] = e_in[2 * h + par_rem]
    loads[5].wait()
    p_snd[...] = p_in[snd_rem]

    pl.semaphore_wait(barrier, 53)

    def send_partner(d, carry):
        remote(partbuf.at[mom], partbuf.at[mom], 0, (src, z, (mom + d) % 4)).start()
        return carry

    lax.fori_loop(1, 4, send_partner, 0)

    def send_e1(d, carry):
        i = (me + d) % 32
        rows = pl.ds(pl.multiple_of(32 * i, 32), 32)
        remote(e_snd.at[:, rows, :], e1.at[me], 1, (i // 4, z, i % 4)).start()
        return carry

    lax.fori_loop(1, 32, send_e1, 0)
    e1[me] = e_snd[:, own_rows, :]

    for plane in range(2):

        def send_p1(d, carry):
            j = (u + d) % 16
            rows = pl.ds(pl.multiple_of(16 * j, 16), 16)
            remote(
                p_snd.at[plane, rows, :], p1[plane].at[u], 2 + plane, (j // 2, z_rem, 2 * (j % 2) + e)
            ).start()
            return carry

        lax.fori_loop(0, 16, send_p1, 0)

    eloc[mom] = e_in[2 * c + par_loc]
    own_e = remote(eloc.at[mom], eloc.at[mom], 4, other_core)
    own_e.start()
    el_snd[...] = e_in[2 * (1 - c) + par_loc]
    for s in range(4):
        pl_snd[:, s] = p_in[snd_loc, :, :, pl.ds(128 * s, 128)]

    arrived(partbuf.at[pl.ds(0, 3)], 0)
    partners = [partbuf[o, 0, 0] for o in range(4)]
    arrived(e1.at[pl.ds(0, 31)], 1)

    def rem_op(core, a):
        return jnp.where(is_a, jnp.where(core == 0, partners[2 * a], partners[2 * a + 1]), core + 2 * a)

    def pick_e(i, a):
        block = (i // 2 + shift) % 16
        return e1[(block // 2) * 4 + rem_op(i % 2, a), block % 2]

    def send_e2(d, carry):
        i = (me + d) % 32
        for a in range(2):
            e2s[i, a] = pick_e(i, a)
        remote(e2s.at[i], erem.at[:, own_rows, :], 5, (i // 4, z, i % 4)).start()
        return carry

    lax.fori_loop(1, 32, send_e2, 0)
    for a in range(2):
        erem[a, own_rows, :] = pick_e(me, a)

    direct_p = remote(pl_snd, pn.at[pl.ds(0, 2), :, half, :], 6, (src, z_loc, mom))
    direct_p.start()
    cross_e = remote(el_snd, eloc.at[mom], 7, other_chip)
    cross_e.start()

    for plane in range(2):
        arrived(p1[plane], 2 + plane)

        def send_p2(d, carry):
            j = (u + d) % 16
            p2s[plane, j] = p1[plane][(j + shift) % 16]
            remote(
                p2s.at[plane, j], prem.at[plane, own_strip, :], 8 + plane, (j // 2, z, 2 * (j % 2) + e)
            ).start()
            return carry

        lax.fori_loop(1, 16, send_p2, 0)
        prem[plane, own_strip, :] = p1[plane][(u + shift) % 16]

    cross_e.wait_recv()
    from_chip = eloc.at[2 * (1 - c) + e]
    pass_e = remote(from_chip, from_chip, 10, other_core)
    pass_e.start()
    direct_p.wait_recv()
    own_part = pn.at[pl.ds(0, 2), :, half, :]
    pass_p = remote(own_part, own_part, 11, other_core)
    pass_p.start()
    own_e.wait_recv()
    pass_e.wait_recv()
    pass_p.wait_recv()

    pn[2] = -pn[0]
    pn[3] = -pn[1]

    def times_local(step, carry):
        a, s = step // 4, step % 4
        op = jnp.where(is_a, e + 2 * a, partbuf[e + 2 * a, 0, 0])
        left_re, left_im, right = [], [], []
        for r in range(4):
            code = gam_ref[op, r]
            pattern = tab_ref[5 * code]
            power = tab_ref[5 * code + 1 + s]
            left_re.append(pn[(4 - power) % 4, s ^ pattern])
            left_im.append(pn[(5 - power) % 4, s ^ pattern])
            right.append(
                jnp.concatenate([eloc[op, pl.ds(256 * r, 128), :], eloc[op, pl.ds(256 * r + 128, 128), :]], axis=1)
            )
        right = jnp.concatenate(right, axis=0)
        by_re = jnp.dot(jnp.concatenate(left_re, axis=1), right, preferred_element_type=jnp.float32)
        by_im = jnp.dot(jnp.concatenate(left_im, axis=1), right, preferred_element_type=jnp.float32)
        lanes = pl.ds(pl.multiple_of(128 * s, 128), 128)
        fbuf[a, pl.ds(0, 512), lanes] = (by_re[:, :128] - by_im[:, 128:]).astype(jnp.bfloat16)
        fbuf[a, pl.ds(512, 512), lanes] = (by_re[:, 128:] + by_im[:, :128]).astype(jnp.bfloat16)
        return carry

    lax.fori_loop(0, 8, times_local, 0)

    arrived(e1.at[pl.ds(0, 31)], 5)

    def turn(step, carry):
        rows = pl.ds(pl.multiple_of(128 * (step % 8), 128), 128)
        ptr[step] = erem[step // 8, rows, :].astype(jnp.float32).T
        return carry

    lax.fori_loop(0, 16, turn, 0)

    passes = []
    for plane in range(2):
        arrived(p1[plane].at[pl.ds(0, 15)], 8 + plane)
        own_rem = prem.at[plane, half, :]
        passes.append(remote(own_rem, own_rem, 12 + plane, other_core))
        passes[plane].start()
        passes[plane].wait_recv()

        def times_remote(step, carry):
            a, cols = step // 2, pl.ds(pl.multiple_of(256 * (step % 2), 256), 256)
            product = jnp.dot(fbuf[a], prem[plane, :, cols], preferred_element_type=jnp.float32)
            for s in range(2):
                lanes = slice(128 * s, 128 * s + 128)
                spin = 2 * (step % 2) + s
                if plane == 0:
                    nbuf[a, 0, spin] = product[:512, lanes]
                    nbuf[a, 1, spin] = product[512:, lanes]
                else:
                    nbuf[a, 0, spin] -= product[512:, lanes]
                    nbuf[a, 1, spin] += product[:512, lanes]
            return carry

        lax.fori_loop(0, 4, times_remote, 0)

    lane = lax.broadcasted_iota(jnp.int32, (8, 128), 1)
    for a in range(2):
        op = rem_op(e, a)

        def close(r, carry):
            acc_re, acc_im = carry
            code = gam_ref[op, r]
            pattern = tab_ref[5 * code]
            sum_re = jnp.zeros((128, 128), jnp.float32)
            sum_im = jnp.zeros((128, 128), jnp.float32)
            for s in range(4):
                power = tab_ref[5 * code + 1 + s]
                ca = jnp.where(power == 0, 1.0, jnp.where(power == 2, -1.0, 0.0))
                cb = jnp.where(power == 1, 1.0, jnp.where(power == 3, -1.0, 0.0))
                n_re = nbuf[a, 0, s ^ pattern, pl.ds(128 * s, 128), :]
                n_im = nbuf[a, 1, s ^ pattern, pl.ds(128 * s, 128), :]
                sum_re += ca * n_re - cb * n_im
                sum_im += ca * n_im + cb * n_re
            t_re, t_im = ptr[8 * a + 2 * r], ptr[8 * a + 2 * r + 1]
            return acc_re + sum_re * t_re - sum_im * t_im, acc_im + sum_re * t_im + sum_im * t_re

        zero = jnp.zeros((128, 128), jnp.float32)
        acc_re, acc_im = lax.fori_loop(0, 4, close, (zero, zero))
        res[a] = jnp.where(
            lane == 2 * k, jnp.sum(acc_re) / 512, jnp.where(lane == 2 * k + 1, jnp.sum(acc_im) / 512, 0.0)
        )

    def send_r1(d, carry):
        remote(res, r1.at[z], 14, (src, (z + d) % 8, mom)).start()
        return carry

    lax.fori_loop(1, 8, send_r1, 0)
    r1[z] = res[...]
    arrived(r1.at[pl.ds(0, 7)], 14)
    row = lax.broadcasted_iota(jnp.int32, (8, 128), 0)
    for a in range(2):
        tile = jnp.zeros((8, 128), jnp.float32)
        for plane in range(8):
            tile = jnp.where(row == plane, r1[plane, a], tile)
        t2[a] = tile

    def send_r2(d, carry):
        j = (u + d) % 16
        remote(t2.at[j % 2], r2.at[u], 15, (j // 2, z, 2 * (j % 2) + e)).start()
        return carry

    lax.fori_loop(1, 16, send_r2, 0)
    r2[u] = t2[c]
    arrived(r2.at[pl.ds(0, 15)], 15)

    odd_planes = (row == 0) | (row == 3) | (row == 5) | (row == 6)

    def gather(v, carry):
        even_row = jnp.sum(jnp.where(odd_planes, 0.0, r2[v]), axis=0, keepdims=True)
        tile = jnp.zeros((8, 128), jnp.float32)
        for kk in range(NSEP):
            sep_k = sep_ref[kk]
            block = ((2 * v + 1 + sep_k - ((1 + sep_k) & 1)) // 2) % 16
            tile += jnp.where(row == ROLE_B_PLANES[kk], r2[block], 0.0)
        odd_row = jnp.sum(tile, axis=0, keepdims=True)
        out_ref[v] = jnp.concatenate([even_row, odd_row], axis=0)
        return carry

    lax.fori_loop(0, 16, gather, 0)

    left(partbuf.at[pl.ds(0, 3)], 0)
    left(e1.at[pl.ds(0, 31)], 1)
    left(e1.at[pl.ds(0, 31)], 5)
    for plane in range(2):
        left(p1[plane], 2 + plane)
        left(p1[plane].at[pl.ds(0, 15)], 8 + plane)
    for copy in [own_e, cross_e, direct_p, pass_e, pass_p] + passes:
        copy.wait_send()
    left(r1.at[pl.ds(0, 7)], 14)
    left(r2.at[pl.ds(0, 15)], 15)


def shards(peram_blocks, projections, gamma_index, partner, separations):
    bf, f32 = jnp.bfloat16, jnp.float32
    anywhere = pl.BlockSpec(memory_space=pl.ANY)
    out = pl.pallas_call(
        body,
        out_shape=jax.ShapeDtypeStruct((16, 2, 128), f32),
        in_specs=[anywhere] * 6,
        out_specs=pl.BlockSpec(memory_space=pltpu.VMEM),
        scratch_shapes=[
            pltpu.SMEM((4,), jnp.int32),
            pltpu.SMEM((4, 4), jnp.int32),
            pltpu.SMEM((1,), jnp.int32),
            pltpu.SMEM((80,), jnp.int32),
            pltpu.VMEM((4, 1024, 128), bf),
            pltpu.VMEM((2, 2, 256, 512), bf),
            pltpu.VMEM((2, 1024, 128), bf),
            pltpu.VMEM((2, 256, 512), bf),
            pltpu.VMEM((2, 4, 256, 128), bf),
            pltpu.VMEM((1024, 128), bf),
            pltpu.VMEM((32, 2, 32, 128), bf),
            pltpu.VMEM((16, 16, 512), bf),
            pltpu.VMEM((16, 16, 512), bf),
            pltpu.VMEM((32, 2, 32, 128), bf),
            pltpu.VMEM((2, 16, 16, 512), bf),
            pltpu.VMEM((4, 1024, 128), bf),
            pltpu.VMEM((2, 1024, 128), bf),
            pltpu.VMEM((2, 512, 512), bf),
            pltpu.VMEM((4, 4, 512, 128), bf),
            pltpu.VMEM((2, 1024, 512), bf),
            pltpu.VMEM((2, 2, 4, 512, 128), f32),
            pltpu.VMEM((16, 128, 128), f32),
            pltpu.VMEM((4, 8, 128), jnp.int32),
            pltpu.VMEM((2, 8, 128), f32),
            pltpu.VMEM((8, 2, 8, 128), f32),
            pltpu.VMEM((2, 8, 128), f32),
            pltpu.VMEM((16, 8, 128), f32),
            pltpu.SemaphoreType.DMA((6,)),
            pltpu.SemaphoreType.DMA((16,)),
            pltpu.SemaphoreType.DMA((16,)),
        ],
        compiler_params=pltpu.CompilerParams(collective_id=0, has_side_effects=True, vmem_limit_bytes=48 * 1024 * 1024),
    )(
        separations,
        gamma_index,
        partner,
        jnp.asarray(gamma_table()),
        peram_blocks,
        projections.reshape(4, 1024, 128),
    )
    return out[:, :, : 2 * NSEP].reshape(32, NSEP, 1, 2)


def solution(mesh):
    placed = (
        P("src", "snk", None, None, None),
        P("src", "mom", None, None, None, None),
        P(),
        P("mom"),
        P(),
    )
    return jax.shard_map(
        shards, mesh=mesh, in_specs=placed, out_specs=P(None, None, "mom", None), check_vma=False
    )
```

time: 76.8 us -> 76.1 us (level)
  no operation moved by 1% of the time
where the time goes in v2:
time: 76.1 us; the launch traced here: 75.9 us
  Pallas kernels  69.1 us (91%)
  local copies, waits for them, and re-layouts  6.19 us (8%)
    pallas_call x1, Pallas kernels, shards(): pl.pallas_call(body, out_shape=jax.ShapeDtypeStruct((16, 2, 128), f32), i...  69.1 us
    unnamed x10, local copies, waits for them, and re-layouts  5.4 us

profile of v2, /device:TPU:1, one launch (start us, length us, event | category | flops | bytes accessed | tf_op | source)
XLA Modules:
  0.0 75.9 jit_solution(2433134234812216250)
XLA Ops:
  0.7 0.0 copy-start
  0.7 2.2 %copy-done = bf16[4,1,2,512,512]{4,3,2,1,0:T(8,128)(2,1)S(1)} copy-done((bf16[4,1,2,512,512]{4,3,2,1,0:T(8,128)(2,1)S(1)}, bf16[4,1,2,512,512]{4,3,2,1,0:T(8,128)(2,1)}, u32[]{:S(2)}) %copy-start) | copy-done | bytes 4194328
  2.8 0.0 copy-start.1
  2.8 1.2 %copy-done.1 = bf16[4,1,4,2,128,128]{5,4,3,2,1,0:T(8,128)(2,1)S(1)} copy-done((bf16[4,1,4,2,128,128]{5,4,3,2,1,0:T(8,128)(2,1)S(1)}, bf16[4,1,4,2,128,128]{5,4,3,2,1,0:T(8,128)(2,1)}, u32[]{:S(2)}) %copy-start.1) | copy-done | bytes 1048600
  4.1 0.0 copy-start.2
  4.1 0.7 copy-done.2
  4.7 0.0 copy-start.3
  4.8 0.7 copy-done.3
  5.4 0.0 copy-start.4
  5.4 0.7 copy-done.4
  6.1 69.1 %shard_map.64 = f32[16,2,128]{2,1,0:T(2,128)S(1)} custom-call(s32[4]{0:T(128)S(1)} %copy-done.3, s32[4,4]{1,0:T(4,128)S(1)} %copy-done.2, s32[1]{0:T(128)S(6)} %copy.12.part_hbm, s32[80]{0:T(128)S(1)} %copy-done.4, bf16[4,1,2,512,512]{4,3,2,1,0:T(8,128)(2,1)S(1)} %copy-done, bf16[4,1024,128]{2,1,0:T(8,128)(2,1)S(1)} %bitcast.2), custom_call_target="tpu_custom_call" | custom-call | tf_op jit(solution)/shard_map/pallas_call | solution.py:350
  75.1 0.1 reshape.8
  75.3 0.7 copy.9
Async XLA Ops:
  0.7 2.2 %copy-start = (bf16[4,1,2,512,512]{4,3,2,1,0:T(8,128)(2,1)S(1)}, bf16[4,1,2,512,512]{4,3,2,1,0:T(8,128)(2,1)}, u32[]{:S(2)}) copy-start(bf16[4,1,2,512,512]{4,3,2,1,0:T(8,128)(2,1)} %p_ref.1) | copy-start | bytes 12582916
  2.8 1.2 %copy-start.1 = (bf16[4,1,4,2,128,128]{5,4,3,2,1,0:T(8,128)(2,1)S(1)}, bf16[4,1,4,2,128,128]{5,4,3,2,1,0:T(8,128)(2,1)}, u32[]{:S(2)}) copy-start(bf16[4,1,4,2,128,128]{5,4,3,2,1,0:T(8,128)(2,1)} %param.7) | copy-start | bytes 3145732
  4.1 0.7 copy-start.2
  4.7 0.7 copy-start.3
  5.4 0.7 copy-start.4

commit v3 on v2

--- a/solution.py
+++ b/solution.py
@@ -34,7 +34,7 @@
 def body(
     sep_hbm, gam_hbm, part_hbm, tab_hbm, p_ref, e_ref, out_ref,
     sep_ref, gam_ref, part_ref, tab_ref,
-    e_in, p_in, e_snd, p_snd, pl_snd, el_snd, e1, p1_re, p1_im, e2s, p2s, eloc, erem, prem, pn,
+    e_in, p_in, e_snd, p_snd, pl_snd, el_snd, e1, p1_re, p1_im, e2s, p2s, eloc, erem, ploc, pmine, pother,
     fbuf, nbuf, ptr, partbuf, res, r1, t2, r2, lsem, ssem, rsem,
 ):
     src, z, mom = lax.axis_index("src"), lax.axis_index("snk"), lax.axis_index("mom")
@@ -63,7 +63,7 @@
     other_chip = (src, z, 2 * (1 - c) + e)
     half = pl.ds(pl.multiple_of(256 * e, 256), 256)
     own_rows = pl.ds(pl.multiple_of(32 * me, 32), 32)
-    own_strip = pl.ds(pl.multiple_of(256 * e + 16 * u, 16), 16)
+    own_strip = pl.ds(pl.multiple_of(16 * u, 16), 16)
 
     loads = [
         pltpu.make_async_copy(one, two, lsem.at[index])
@@ -117,7 +117,8 @@
     for h in range(2):
         e_snd[h] = e_in[2 * h + par_rem]
     loads[5].wait()
-    p_snd[...] = p_in[snd_rem]
+    for s in range(4):
+        p_snd[:, s] = p_in[snd_rem, :, :, pl.ds(128 * s, 128)]
 
     pl.semaphore_wait(barrier, 53)
 
@@ -142,7 +143,7 @@
             j = (u + d) % 16
             rows = pl.ds(pl.multiple_of(16 * j, 16), 16)
             remote(
-                p_snd.at[plane, rows, :], p1[plane].at[u], 2 + plane, (j // 2, z_rem, 2 * (j % 2) + e)
+                p_snd.at[plane, :, rows, :], p1[plane].at[u], 2 + plane, (j // 2, z_rem, 2 * (j % 2) + e)
             ).start()
             return carry
 
@@ -152,8 +153,7 @@
     own_e = remote(eloc.at[mom], eloc.at[mom], 4, other_core)
     own_e.start()
     el_snd[...] = e_in[2 * (1 - c) + par_loc]
-    for s in range(4):
-        pl_snd[:, s] = p_in[snd_loc, :, :, pl.ds(128 * s, 128)]
+    pl_snd[...] = p_in[snd_loc]
 
     arrived(partbuf.at[pl.ds(0, 3)], 0)
     partners = [partbuf[o, 0, 0] for o in range(4)]
@@ -177,10 +177,14 @@
     for a in range(2):
         erem[a, own_rows, :] = pick_e(me, a)
 
-    direct_p = remote(pl_snd, pn.at[pl.ds(0, 2), :, half, :], 6, (src, z_loc, mom))
-    direct_p.start()
     cross_e = remote(el_snd, eloc.at[mom], 7, other_chip)
     cross_e.start()
+    chunks = [pl.ds(pl.multiple_of(256 * e + 128 * i, 128), 128) for i in range(2)]
+    direct_p = []
+    for i in range(2):
+        part = pl_snd.at[:, pl.ds(128 * i, 128), :]
+        direct_p.append(remote(part, ploc.at[:, chunks[i], :], 16 + i, (src, z_loc, mom)))
+        direct_p[i].start()
 
     for plane in range(2):
         arrived(p1[plane], 2 + plane)
@@ -189,87 +193,109 @@
             j = (u + d) % 16
             p2s[plane, j] = p1[plane][(j + shift) % 16]
             remote(
-                p2s.at[plane, j], prem.at[plane, own_strip, :], 8 + plane, (j // 2, z, 2 * (j % 2) + e)
+                p2s.at[plane, j], pmine.at[plane, :, own_strip, :], 8 + plane, (j // 2, z, 2 * (j % 2) + e)
             ).start()
             return carry
 
         lax.fori_loop(1, 16, send_p2, 0)
-        prem[plane, own_strip, :] = p1[plane][(u + shift) % 16]
+        pmine[plane, :, own_strip, :] = p1[plane][(u + shift) % 16]
 
     cross_e.wait_recv()
     from_chip = eloc.at[2 * (1 - c) + e]
     pass_e = remote(from_chip, from_chip, 10, other_core)
     pass_e.start()
-    direct_p.wait_recv()
-    own_part = pn.at[pl.ds(0, 2), :, half, :]
-    pass_p = remote(own_part, own_part, 11, other_core)
-    pass_p.start()
+    pass_p, pass_r = [], []
+
+    def pass_local(i):
+        direct_p[i].wait_recv()
+        part = ploc.at[:, chunks[i], :]
+        pass_p.append(remote(part, part, 11 + i, other_core))
+        pass_p[i].start()
+
+    pass_local(0)
     own_e.wait_recv()
     pass_e.wait_recv()
-    pass_p.wait_recv()
-
-    pn[2] = -pn[0]
-    pn[3] = -pn[1]
-
-    def times_local(step, carry):
-        a, s = step // 4, step % 4
-        op = jnp.where(is_a, e + 2 * a, partbuf[e + 2 * a, 0, 0])
-        left_re, left_im, right = [], [], []
-        for r in range(4):
-            code = gam_ref[op, r]
-            pattern = tab_ref[5 * code]
-            power = tab_ref[5 * code + 1 + s]
-            left_re.append(pn[(4 - power) % 4, s ^ pattern])
-            left_im.append(pn[(5 - power) % 4, s ^ pattern])
-            right.append(
-                jnp.concatenate([eloc[op, pl.ds(256 * r, 128), :], eloc[op, pl.ds(256 * r + 128, 128), :]], axis=1)
-            )
-        right = jnp.concatenate(right, axis=0)
-        by_re = jnp.dot(jnp.concatenate(left_re, axis=1), right, preferred_element_type=jnp.float32)
-        by_im = jnp.dot(jnp.concatenate(left_im, axis=1), right, preferred_element_type=jnp.float32)
-        lanes = pl.ds(pl.multiple_of(128 * s, 128), 128)
-        fbuf[a, pl.ds(0, 512), lanes] = (by_re[:, :128] - by_im[:, 128:]).astype(jnp.bfloat16)
-        fbuf[a, pl.ds(512, 512), lanes] = (by_re[:, 128:] + by_im[:, :128]).astype(jnp.bfloat16)
-        return carry
-
-    lax.fori_loop(0, 8, times_local, 0)
-
-    arrived(e1.at[pl.ds(0, 31)], 5)
+
+    def loc_op(a):
+        return jnp.where(is_a, e + 2 * a, partbuf[e + 2 * a, 0, 0])
 
     def turn(step, carry):
         rows = pl.ds(pl.multiple_of(128 * (step % 8), 128), 128)
-        ptr[step] = erem[step // 8, rows, :].astype(jnp.float32).T
+        ptr[step] = eloc[loc_op(step // 8), rows, :].astype(jnp.float32).T
         return carry
 
     lax.fori_loop(0, 16, turn, 0)
 
-    passes = []
+    arrived(e1.at[pl.ds(0, 31)], 5)
     for plane in range(2):
         arrived(p1[plane].at[pl.ds(0, 15)], 8 + plane)
-        own_rem = prem.at[plane, half, :]
-        passes.append(remote(own_rem, own_rem, 12 + plane, other_core))
-        passes[plane].start()
-        passes[plane].wait_recv()
-
-        def times_remote(step, carry):
+        pass_r.append(remote(pmine.at[plane], pother.at[plane], 18 + plane, other_core))
+        pass_r[plane].start()
+
+    def times_projections(block, which):
+        block[2] = -block[0]
+        block[3] = -block[1]
+
+        def product(step, carry):
+            a, s = step // 4, step % 4
+            own_rem_op = jnp.where(is_a, partbuf[e + 2 * a, 0, 0], e + 2 * a)
+            left_re, left_im, right = [], [], []
+            for r in range(4):
+                code = gam_ref[own_rem_op, r]
+                pattern = tab_ref[5 * code]
+                power = tab_ref[5 * code + 1 + s]
+                left_re.append(block[(4 - power) % 4, s ^ pattern])
+                left_im.append(block[(5 - power) % 4, s ^ pattern])
+                right.append(
+                    jnp.concatenate([erem[a, pl.ds(256 * r, 128), :], erem[a, pl.ds(256 * r + 128, 128), :]], axis=1)
+                )
+            left = jnp.concatenate([jnp.concatenate(left_re, axis=1), jnp.concatenate(left_im, axis=1)], axis=0)
+            both = jnp.dot(left, jnp.concatenate(right, axis=0), preferred_element_type=jnp.float32)
+            lanes = pl.ds(pl.multiple_of(128 * s, 128), 128)
+            re_rows = pl.ds(pl.multiple_of(256 * which, 256), 256)
+            im_rows = pl.ds(pl.multiple_of(256 * which + 512, 256), 256)
+            fbuf[a, re_rows, lanes] = (both[:256, :128] - both[256:, 128:]).astype(jnp.bfloat16)
+            fbuf[a, im_rows, lanes] = (both[:256, 128:] + both[256:, :128]).astype(jnp.bfloat16)
+            return carry
+
+        lax.fori_loop(0, 8, product, 0)
+
+    times_projections(pmine, e)
+    pass_local(1)
+    for copy in pass_r:
+        copy.wait_recv()
+    times_projections(pother, 1 - e)
+
+    for i in range(2):
+        pass_p[i].wait_recv()
+
+        def times_local(step, carry):
             a, cols = step // 2, pl.ds(pl.multiple_of(256 * (step % 2), 256), 256)
-            product = jnp.dot(fbuf[a], prem[plane, :, cols], preferred_element_type=jnp.float32)
+            left = jnp.concatenate([fbuf[a, :, pl.ds(128 * i, 128)], fbuf[a, :, pl.ds(256 + 128 * i, 128)]], axis=1)
+            by = []
+            for plane in range(2):
+                right = jnp.concatenate(
+                    [ploc[plane, pl.ds(128 * i, 128), cols], ploc[plane, pl.ds(256 + 128 * i, 128), cols]], axis=0
+                )
+                by.append(jnp.dot(left, right, preferred_element_type=jnp.float32))
+            n_re = by[0][:512] - by[1][512:]
+            n_im = by[0][512:] + by[1][:512]
             for s in range(2):
                 lanes = slice(128 * s, 128 * s + 128)
                 spin = 2 * (step % 2) + s
-                if plane == 0:
-                    nbuf[a, 0, spin] = product[:512, lanes]
-                    nbuf[a, 1, spin] = product[512:, lanes]
+                if i == 0:
+                    nbuf[a, 0, spin] = n_re[:, lanes]
+                    nbuf[a, 1, spin] = n_im[:, lanes]
                 else:
-                    nbuf[a, 0, spin] -= product[512:, lanes]
-                    nbuf[a, 1, spin] += product[:512, lanes]
+                    nbuf[a, 0, spin] += n_re[:, lanes]
+                    nbuf[a, 1, spin] += n_im[:, lanes]
             return carry
 
-        lax.fori_loop(0, 4, times_remote, 0)
+        lax.fori_loop(0, 4, times_local, 0)
 
     lane = lax.broadcasted_iota(jnp.int32, (8, 128), 1)
     for a in range(2):
-        op = rem_op(e, a)
+        op = loc_op(a)
 
         def close(r, carry):
             acc_re, acc_im = carry
@@ -338,7 +364,7 @@
     for plane in range(2):
         left(p1[plane], 2 + plane)
         left(p1[plane].at[pl.ds(0, 15)], 8 + plane)
-    for copy in [own_e, cross_e, direct_p, pass_e, pass_p] + passes:
+    for copy in [own_e, cross_e, pass_e] + direct_p + pass_p + pass_r:
         copy.wait_send()
     left(r1.at[pl.ds(0, 7)], 14)
     left(r2.at[pl.ds(0, 15)], 15)
@@ -346,7 +372,7 @@
 
 def shards(peram_blocks, projections, gamma_index, partner, separations):
     bf, f32 = jnp.bfloat16, jnp.float32
-    anywhere = pl.BlockSpec(memory_space=pl.ANY)
+    anywhere = pl.BlockSpec(memory_space=pltpu.HBM)
     out = pl.pallas_call(
         body,
         out_shape=jax.ShapeDtypeStruct((16, 2, 128), f32),
@@ -360,18 +386,19 @@
             pltpu.VMEM((4, 1024, 128), bf),
             pltpu.VMEM((2, 2, 256, 512), bf),
             pltpu.VMEM((2, 1024, 128), bf),
+            pltpu.VMEM((2, 4, 256, 128), bf),
             pltpu.VMEM((2, 256, 512), bf),
-            pltpu.VMEM((2, 4, 256, 128), bf),
             pltpu.VMEM((1024, 128), bf),
             pltpu.VMEM((32, 2, 32, 128), bf),
-            pltpu.VMEM((16, 16, 512), bf),
-            pltpu.VMEM((16, 16, 512), bf),
+            pltpu.VMEM((16, 4, 16, 128), bf),
+            pltpu.VMEM((16, 4, 16, 128), bf),
             pltpu.VMEM((32, 2, 32, 128), bf),
-            pltpu.VMEM((2, 16, 16, 512), bf),
+            pltpu.VMEM((2, 16, 4, 16, 128), bf),
             pltpu.VMEM((4, 1024, 128), bf),
             pltpu.VMEM((2, 1024, 128), bf),
             pltpu.VMEM((2, 512, 512), bf),
-            pltpu.VMEM((4, 4, 512, 128), bf),
+            pltpu.VMEM((4, 4, 256, 128), bf),
+            pltpu.VMEM((4, 4, 256, 128), bf),
             pltpu.VMEM((2, 1024, 512), bf),
             pltpu.VMEM((2, 2, 4, 512, 128), f32),
             pltpu.VMEM((16, 128, 128), f32),
@@ -381,10 +408,10 @@
             pltpu.VMEM((2, 8, 128), f32),
             pltpu.VMEM((16, 8, 128), f32),
             pltpu.SemaphoreType.DMA((6,)),
-            pltpu.SemaphoreType.DMA((16,)),
-            pltpu.SemaphoreType.DMA((16,)),
+            pltpu.SemaphoreType.DMA((20,)),
+            pltpu.SemaphoreType.DMA((20,)),
         ],
-        compiler_params=pltpu.CompilerParams(collective_id=0, has_side_effects=True, vmem_limit_bytes=48 * 1024 * 1024),
+        compiler_params=pltpu.CompilerParams(collective_id=0, has_side_effects=True, vmem_limit_bytes=64 * 1024 * 1024 - 65536),
     )(
         separations,
         gamma_index,

time: 76.1 us -> 71 us (0.933)
  local copies, waits for them, and re-layouts: 6.19 us -> 1.51 us
    unnamed x10 -> x0, local copies, waits for them, and re-layouts: 5.4 us -> none
where the time goes in v3:
time: 71 us; the launch traced here: 70.8 us
  Pallas kernels  68.6 us (97%)
  local copies, waits for them, and re-layouts  1.51 us (2%)
    pallas_call x1, Pallas kernels, shards(): pl.pallas_call(body, out_shape=jax.ShapeDtypeStruct((16, 2, 128), f32), i...  68.6 us
    reshape x2, local copies, waits for them, and re-layouts, shards(): return out[:, :, :2 * NSEP].reshape(32, NSEP, 1, 2)  1.51 us

profile of v3, /device:TPU:1, one launch (start us, length us, event | category | flops | bytes accessed | tf_op | source)
XLA Modules:
  0.0 70.8 jit_solution(4958081487780119438)
XLA Ops:
  0.7 68.6 %shard_map.64 = f32[16,2,128]{2,1,0:T(2,128)} custom-call(s32[4]{0:T(128)} %sep_hbm.1, s32[4,4]{1,0:T(4,128)} %gam_hbm.1, s32[1]{0:T(128)S(6)} %copy.12.part_hbm, s32[80]{0:T(128)} %constant.2.clone.tab_hbm, bf16[4,1,2,512,512]{4,3,2,1,0:T(8,128)(2,1)} %p_ref.1, bf16[4,1024,128]{2,1,0:T(8,128)(2,1)} %bitcast.2), custom_call_target="tpu_custom_call" | custom-call | tf_op jit(solution)/shard_map/pallas_call | solution.py:376
  69.3 0.8 %reshape.8 = f32[32,4,1,2]{3,1,0,2:T(4,128)S(1)} reshape(f32[16,2,8]{2,1,0:T(2,128)} %bitcast.3) | data formatting | bytes 2048 | tf_op jit(solution)/shard_map/reshape | solution.py:423
  70.1 0.7 copy.9

commit v4 on v3

v4 whole, which is shorter than its diff:
```python
import functools

import jax
import jax.numpy as jnp
import numpy as np
from jax import lax
from jax.experimental import pallas as pl
from jax.experimental.pallas import tpu as pltpu
from jax.sharding import PartitionSpec as P

MESH = pl.DeviceIdType.MESH
NSEP = 4


def gamma_table():
    unit = np.eye(4, dtype=complex)
    one = np.array([[0, 0, 0, 1j], [0, 0, 1j, 0], [0, -1j, 0, 0], [-1j, 0, 0, 0]])
    two = np.array([[0, 0, 0, -1], [0, 0, 1, 0], [0, 1, 0, 0], [-1, 0, 0, 0]], dtype=complex)
    three = np.array([[0, 0, 1j, 0], [0, 0, 0, -1j], [-1j, 0, 0, 0], [0, 1j, 0, 0]])
    four = np.array([[0, 0, 1, 0], [0, 0, 0, 1], [1, 0, 0, 0], [0, 1, 0, 0]], dtype=complex)
    rows = []
    for code in range(16):
        value = unit
        for position, factor in enumerate((one, two, three, four)):
            if code >> position & 1:
                value = value @ factor
        pattern = int(np.flatnonzero(np.abs(value[:, 0]))[0])
        powers = [(1, 1j, -1, -1j).index(complex(value[s ^ pattern, s])) for s in range(4)]
        rows.append([pattern] + powers)
    return np.array(rows, dtype=np.int32).reshape(-1)


def body(
    sep_hbm, gam_hbm, part_hbm, tab_hbm, p_ref, e_ref, out_ref,
    sep_ref, gam_ref, part_ref, tab_ref,
    e_in, p_in, e_snd, p_snd, pl_snd, el_snd, e1, p1_re, p1_im, e2s, p2s, eloc, erem_0, erem_1, ploc, pmine, pother,
    fbuf, ptr, elt, partbuf, res, r1, t2, r2, lsem, ssem, rsem,
):
    src, z, mom = lax.axis_index("src"), lax.axis_index("snk"), lax.axis_index("mom")
    c, e = mom >> 1, mom & 1
    u = 2 * src + c
    me = 4 * src + mom
    k = (z + 2) & 3
    z_even = 1 - (z & 1)
    z_rem = (z + 2 + 4 * z_even) & 7
    z_loc = (z + 6 + 4 * z_even) & 7
    p1 = (p1_re, p1_im)
    erem = (erem_0, erem_1)

    def remote(src_ref, dst_ref, index, target):
        return pltpu.make_async_remote_copy(
            src_ref=src_ref, dst_ref=dst_ref, send_sem=ssem.at[index], recv_sem=rsem.at[index],
            device_id=target, device_id_type=MESH,
        )

    def arrived(ref, index):
        pltpu.make_async_copy(ref, ref, rsem.at[index]).wait()

    def left(ref, index):
        pltpu.make_async_copy(ref, ref, ssem.at[index]).wait()

    def near(d):
        flip = (d >> 2) & 1
        column = ((src >> 1) + d) & 3
        return 2 * column + ((src & 1) ^ flip), c ^ flip

    other_core = (src, z, 2 * c + 1 - e)
    other_chip = (src, z, 2 * (1 - c) + e)
    half = pl.ds(pl.multiple_of(256 * e, 256), 256)
    own_rows = pl.ds(pl.multiple_of(32 * me, 32), 32)
    own_strip = pl.ds(pl.multiple_of(16 * u, 16), 16)

    loads = [
        pltpu.make_async_copy(one, two, lsem.at[index])
        for index, (one, two) in enumerate(
            (
                (part_hbm, part_ref),
                (sep_hbm, sep_ref),
                (gam_hbm, gam_ref),
                (tab_hbm, tab_ref),
                (e_ref, e_in),
                (p_ref.at[:, 0, :, half, :], p_in),
            )
        )
    ]
    for load in loads:
        load.start()

    barrier = pltpu.get_barrier_semaphore()

    def greet(target):
        pl.semaphore_signal(barrier, inc=1, device_id=target, device_id_type=MESH)

    def greet_blocks(d, carry):
        there, chip = near(d)
        greet((there, z_loc, 2 * chip + e))
        return carry

    def greet_plane(d, carry):
        i = (me + d) & 31
        greet((i >> 2, z, i & 3))
        return carry

    lax.fori_loop(0, 8, greet_blocks, 0)
    greet((src, z_rem, mom))
    for d in (1, 3, 4, 5, 7):
        greet((src, (z + d) & 7, mom))
    lax.fori_loop(1, 32, greet_plane, 0)

    for load in loads[:5]:
        load.wait()
    sep = sep_ref[k]
    odd = sep & 1
    is_a = ((z + (z >> 1) + (z >> 2)) & 1) == 1
    shift = jnp.where(is_a, sep >> 1, 16 - ((sep + 1) >> 1))
    par_loc = jnp.where(is_a, 0, (1 + odd) & 1)
    par_rem = jnp.where(is_a, odd, 1)
    time = (2 * u + jnp.where(is_a, 0, par_loc - sep)) & 31
    odd_own = sep_ref[z & 3] & 1
    snd_rem = jnp.where(z < NSEP, 1, odd_own)
    snd_loc = jnp.where(z < NSEP, 0, (1 + odd_own) & 1)
    partbuf[mom] = jnp.full((8, 128), part_ref[0], jnp.int32)
    for h in range(2):
        e_snd[h] = e_in[2 * h + par_rem]
    eloc[mom] = e_in[2 * c + par_loc]
    el_snd[...] = e_in[2 * (1 - c) + par_loc]
    loads[5].wait()
    for h in range(2):
        for s in range(4):
            p_snd[:, h, s] = p_in[2 * h + snd_rem, :, :, pl.ds(128 * s, 128)]
    pl_snd[...] = p_in[2 * c + snd_loc]

    pl.semaphore_wait(barrier, 45)

    def send_partner(d, carry):
        remote(partbuf.at[mom], partbuf.at[mom], 0, (src, z, (mom + d) & 3)).start()
        return carry

    lax.fori_loop(1, 4, send_partner, 0)

    def send_e1(d, carry):
        i = (me + d) & 31
        rows = pl.ds(pl.multiple_of(32 * i, 32), 32)
        remote(e_snd.at[:, rows, :], e1.at[me], 1, (i >> 2, z, i & 3)).start()
        return carry

    lax.fori_loop(1, 32, send_e1, 0)

    for plane in range(2):

        def send_p1(d, carry):
            there, chip = near(d)
            rows = pl.ds(pl.multiple_of(16 * (2 * there + chip), 16), 16)
            h = d >> 3
            remote(
                p_snd.at[plane, h, :, rows, :], p1[plane].at[2 * src + h], 2 + plane, (there, z_rem, 2 * chip + e)
            ).start()
            return carry

        lax.fori_loop(0, 16, send_p1, 0)

    own_e = remote(eloc.at[mom], eloc.at[mom], 4, other_core)
    own_e.start()
    cross_e = remote(el_snd, eloc.at[mom], 7, other_chip)
    cross_e.start()
    e1[me] = e_snd[:, own_rows, :]

    arrived(partbuf.at[pl.ds(0, 3)], 0)
    partners = [partbuf[o, 0, 0] for o in range(4)]
    arrived(e1.at[pl.ds(0, 31)], 1)

    def pick_e(i, a):
        block = ((i >> 1) + shift) & 15
        op = jnp.where(is_a, jnp.where((i & 1) == 0, partners[2 * a], partners[2 * a + 1]), (i & 1) + 2 * a)
        return e1[(block >> 1) * 4 + op, block & 1]

    def spread_e2(a):
        def send_e2(d, carry):
            i = (me + d) & 31
            e2s[a, i] = pick_e(i, a)
            remote(e2s.at[a, i], erem[a].at[own_rows, :], 5 + a, (i >> 2, z, i & 3)).start()
            return carry

        lax.fori_loop(1, 32, send_e2, 0)
        erem[a][own_rows, :] = pick_e(me, a)

    spread_e2(0)

    chunks = [pl.ds(pl.multiple_of(256 * e + 128 * i, 128), 128) for i in range(2)]
    direct_p = []
    for i in range(2):
        part = pl_snd.at[:, pl.ds(128 * i, 128), :]
        direct_p.append(remote(part, ploc.at[:, chunks[i], :], 17 + i, (src, z_loc, mom)))
        direct_p[i].start()

    for plane in range(2):
        arrived(p1[plane], 2 + plane)

        def send_p2(d, carry):
            j = (u + d) & 15
            p2s[plane, j] = p1[plane][(j + shift) & 15]
            remote(
                p2s.at[plane, j], pmine.at[plane, :, own_strip, :], 8 + plane, (j >> 1, z, 2 * (j & 1) + e)
            ).start()
            return carry

        lax.fori_loop(1, 16, send_p2, 0)
        pmine[plane, :, own_strip, :] = p1[plane][(u + shift) & 15]
    spread_e2(1)

    cross_e.wait_recv()
    from_chip = eloc.at[2 * (1 - c) + e]
    pass_e = remote(from_chip, from_chip, 10, other_core)
    pass_e.start()
    pass_p, pass_r = [], []

    def pass_local(i):
        direct_p[i].wait_recv()
        part = ploc.at[:, chunks[i], :]
        pass_p.append(remote(part, part, 11 + i, other_core))
        pass_p[i].start()

    own_e.wait_recv()
    pass_e.wait_recv()

    def loc_op(a):
        return jnp.where(is_a, e + 2 * a, partbuf[e + 2 * a, 0, 0])

    def turn(step, carry):
        rows = pl.ds(pl.multiple_of(128 * (step & 7), 128), 128)
        ptr[step] = eloc[loc_op(step >> 3), rows, :].astype(jnp.float32).T
        return carry

    lax.fori_loop(0, 16, turn, 0)

    def build(step, carry):
        a, s = step >> 2, step & 3
        op = loc_op(a)
        sum_re = [jnp.zeros((128, 128), jnp.float32) for _ in range(4)]
        sum_im = [jnp.zeros((128, 128), jnp.float32) for _ in range(4)]
        for r in range(4):
            code = gam_ref[op, r]
            pattern = tab_ref[5 * code]
            power = tab_ref[5 * code + 1 + s]
            ca = jnp.where(power == 0, 1.0, jnp.where(power == 2, -1.0, 0.0))
            cb = jnp.where(power == 1, 1.0, jnp.where(power == 3, -1.0, 0.0))
            t_re, t_im = ptr[8 * a + 2 * r], ptr[8 * a + 2 * r + 1]
            v_re = ca * t_re - cb * t_im
            v_im = ca * t_im + cb * t_re
            for s_left in range(4):
                here = jnp.where((s ^ pattern) == s_left, 1.0, 0.0)
                sum_re[s_left] += here * v_re
                sum_im[s_left] += here * v_im
        rows = pl.ds(pl.multiple_of(128 * s, 128), 128)
        for s_left in range(4):
            elt[a, 0, rows, pl.ds(128 * s_left, 128)] = sum_re[s_left]
            elt[a, 1, rows, pl.ds(128 * s_left, 128)] = sum_im[s_left]
        return carry

    lax.fori_loop(0, 8, build, 0)

    pass_local(0)
    for plane in range(2):
        arrived(p1[plane].at[pl.ds(0, 15)], 8 + plane)
        pass_r.append(remote(pmine.at[plane], pother.at[plane], 13 + plane, other_core))
        pass_r[plane].start()

    def negate(block):
        block[2] = -block[0]
        block[3] = -block[1]

    def times_projections(block, which, a):
        op = jnp.where(is_a, partbuf[e + 2 * a, 0, 0], e + 2 * a)
        right = jnp.concatenate(
            [
                jnp.concatenate([erem[a][pl.ds(256 * r, 128), :], erem[a][pl.ds(256 * r + 128, 128), :]], axis=1)
                for r in range(4)
            ],
            axis=0,
        )
        re_rows = pl.ds(pl.multiple_of(256 * which, 256), 256)
        im_rows = pl.ds(pl.multiple_of(256 * which + 512, 256), 256)
        for s in range(4):
            left_re, left_im = [], []
            for r in range(4):
                code = gam_ref[op, r]
                pattern = tab_ref[5 * code]
                power = tab_ref[5 * code + 1 + s]
                left_re.append(block[(4 - power) & 3, s ^ pattern])
                left_im.append(block[(5 - power) & 3, s ^ pattern])
            by_re = jnp.dot(jnp.concatenate(left_re, axis=1), right, preferred_element_type=jnp.float32)
            by_im = jnp.dot(jnp.concatenate(left_im, axis=1), right, preferred_element_type=jnp.float32)
            lanes = pl.ds(128 * s, 128)
            fbuf[a, re_rows, lanes] = (by_re[:, :128] - by_im[:, 128:]).astype(jnp.bfloat16)
            fbuf[a, im_rows, lanes] = (by_re[:, 128:] + by_im[:, :128]).astype(jnp.bfloat16)

    lane = lax.broadcasted_iota(jnp.int32, (8, 128), 1)
    row = lax.broadcasted_iota(jnp.int32, (8, 128), 0)

    def close(a):
        def times_local(step, carry):
            acc_re, acc_im = carry
            cols = pl.ds(pl.multiple_of(256 * step, 256), 256)
            by_re = jnp.dot(fbuf[a], ploc[0, :, cols], preferred_element_type=jnp.float32)
            by_im = jnp.dot(fbuf[a], ploc[1, :, cols], preferred_element_type=jnp.float32)
            n_re = by_re[:512] - by_im[512:]
            n_im = by_re[512:] + by_im[:512]
            t_re, t_im = elt[a, 0, :, cols], elt[a, 1, :, cols]
            new_re = n_re * t_re - n_im * t_im
            new_im = n_re * t_im + n_im * t_re
            return (
                acc_re + jnp.sum(new_re.reshape(64, 8, 256), axis=0),
                acc_im + jnp.sum(new_im.reshape(64, 8, 256), axis=0),
            )

        zero = jnp.zeros((8, 256), jnp.float32)
        acc_re, acc_im = lax.fori_loop(0, 2, times_local, (zero, zero))
        mine = jnp.where(row == 2 * k, jnp.sum(acc_re) / 512, jnp.where(row == 2 * k + 1, jnp.sum(acc_im) / 512, 0.0))
        res[a] = jnp.where(lane == time, mine, 0.0)

    arrived(e1.at[pl.ds(0, 31), 0], 5)
    negate(pmine)
    times_projections(pmine, e, 0)
    pass_local(1)
    for copy in pass_r:
        copy.wait_recv()
    negate(pother)
    times_projections(pother, 1 - e, 0)
    for copy in pass_p:
        copy.wait_recv()
    close(0)
    arrived(e1.at[pl.ds(0, 31), 0], 6)
    times_projections(pmine, e, 1)
    times_projections(pother, 1 - e, 1)
    close(1)

    def send_r1(d, carry):
        remote(res, r1.at[z], 15, (src, (z + d) & 7, mom)).start()
        return carry

    lax.fori_loop(1, 8, send_r1, 0)
    r1[z] = res[...]
    arrived(r1.at[pl.ds(0, 7)], 15)
    t2[...] = jnp.sum(r1[...], axis=0)

    def send_r2(d, carry):
        j = (u + d) & 15
        remote(t2.at[j & 1], r2.at[u], 16, (j >> 1, z, 2 * (j & 1) + e)).start()
        return carry

    lax.fori_loop(1, 16, send_r2, 0)
    r2[u] = t2[c]
    arrived(r2.at[pl.ds(0, 15)], 16)
    total = jnp.sum(r2[...], axis=0)
    for kk in range(NSEP):
        out_ref[kk, 0] = total[2 * kk : 2 * kk + 2, :32]

    left(partbuf.at[pl.ds(0, 3)], 0)
    left(e1.at[pl.ds(0, 31)], 1)
    for a in range(2):
        left(e1.at[pl.ds(0, 31), 0], 5 + a)
    for plane in range(2):
        left(p1[plane], 2 + plane)
        left(p1[plane].at[pl.ds(0, 15)], 8 + plane)
    for copy in [own_e, cross_e, pass_e] + direct_p + pass_p + pass_r:
        copy.wait_send()
    left(r1.at[pl.ds(0, 7)], 15)
    left(r2.at[pl.ds(0, 15)], 16)


def shards(peram_blocks, projections, gamma_index, partner, separations):
    bf, f32, i32 = jnp.bfloat16, jnp.float32, jnp.int32
    buffers = [
        ((4, 1024, 128), bf),
        ((4, 2, 256, 512), bf),
        ((2, 1024, 128), bf),
        ((2, 2, 4, 256, 128), bf),
        ((2, 256, 512), bf),
        ((1024, 128), bf),
        ((32, 2, 32, 128), bf),
        ((16, 4, 16, 128), bf),
        ((16, 4, 16, 128), bf),
        ((2, 32, 32, 128), bf),
        ((2, 16, 4, 16, 128), bf),
        ((4, 1024, 128), bf),
        ((1024, 128), bf),
        ((1024, 128), bf),
        ((2, 512, 512), bf),
        ((4, 4, 256, 128), bf),
        ((4, 4, 256, 128), bf),
        ((2, 1024, 512), bf),
        ((16, 128, 128), f32),
        ((2, 2, 512, 512), f32),
        ((4, 8, 128), i32),
        ((2, 8, 128), f32),
        ((8, 2, 8, 128), f32),
        ((2, 8, 128), f32),
        ((16, 8, 128), f32),
    ]
    out = pl.pallas_call(
        body,
        out_shape=jax.ShapeDtypeStruct((NSEP, 1, 2, 32), f32),
        in_specs=[pl.BlockSpec(memory_space=pltpu.HBM)] * 6,
        out_specs=pl.BlockSpec(memory_space=pltpu.VMEM),
        scratch_shapes=[pltpu.SMEM(shape, i32) for shape in ((4,), (4, 4), (1,), (80,))]
        + [pltpu.VMEM(shape, dtype) for shape, dtype in buffers]
        + [pltpu.SemaphoreType.DMA((count,)) for count in (6, 19, 19)],
        compiler_params=pltpu.CompilerParams(
            collective_id=0, has_side_effects=True, vmem_limit_bytes=64 * 1024 * 1024 - 65536
        ),
    )(
        separations,
        gamma_index,
        partner,
        jnp.asarray(gamma_table()),
        peram_blocks,
        projections.reshape(4, 1024, 128),
    )
    return jnp.transpose(out, (3, 0, 1, 2))


def solution(mesh):
    placed = (
        P("src", "snk", None, None, None),
        P("src", "mom", None, None, None, None),
        P(),
        P("mom"),
        P(),
    )
    return jax.shard_map(
        shards, mesh=mesh, in_specs=placed, out_specs=P(None, None, "mom", None), check_vma=False
    )
```

time: 71 us -> 64.2 us (0.904); the launches traced: 70.8 us -> 63.1 us
  Pallas kernels: 68.6 us -> 61.2 us
    pallas_call x1, Pallas kernels: 68.6 us -> 61.2 us  [shards(): pl.pallas_call(body, out_shape=jax.ShapeDtypeStruct((NSEP, 1, 2, 32), f32...]
    reshape x2 -> x0, local copies, waits for them, and re-layouts: 1.51 us -> none  [shards(): return out[:, :, :2 * NSEP].reshape(32, NSEP, 1, 2)]
    unnamed x0 -> x1, local copies, waits for them, and re-layouts: none -> 1.28 us
where the time goes in v4:
time: 64.2 us; the launch traced here: 63.1 us
  Pallas kernels  61.2 us (95%)
  local copies, waits for them, and re-layouts  1.28 us (2%)
  between operations  0.66 us (1%)
    pallas_call x1, Pallas kernels, shards(): pl.pallas_call(body, out_shape=jax.ShapeDtypeStruct((NSEP, 1, 2, 32), f32...  61.2 us

profile of v4, /device:TPU:1, one launch (start us, length us, event | category | flops | bytes accessed | tf_op | source)
XLA Modules:
  0.0 63.1 jit_solution(5544203938137177772)
XLA Ops:
  0.7 61.2 %shard_map.64 = f32[4,1,2,32]{3,2,1,0:T(2,128)} custom-call(s32[4]{0:T(128)} %sep_hbm.1, s32[4,4]{1,0:T(4,128)} %gam_hbm.1, s32[1]{0:T(128)S(6)} %copy.8.part_hbm, s32[80]{0:T(128)} %constant.2.clone.tab_hbm, bf16[4,1,2,512,512]{4,3,2,1,0:T(8,128)(2,1)} %p_ref.1, bf16[4,1024,128]{2,1,0:T(8,128)(2,1)} %bitcast.2), custom_call_target="tpu_custom_call" | custom-call | tf_op jit(solution)/shard_map/pallas_call | solution.py:400
  61.9 1.3 %copy.9 = f32[32,4,1,2]{0,3,2,1:T(2,128)} copy(f32[32,4,1,2]{0,3,2,1:T(2,128)} %bitcast.3) | data formatting | bytes 2048

commit v5 on v4

--- a/solution.py
+++ b/solution.py
@@ -138,16 +138,7 @@
 
     lax.fori_loop(1, 4, send_partner, 0)
 
-    def send_e1(d, carry):
-        i = (me + d) & 31
-        rows = pl.ds(pl.multiple_of(32 * i, 32), 32)
-        remote(e_snd.at[:, rows, :], e1.at[me], 1, (i >> 2, z, i & 3)).start()
-        return carry
-
-    lax.fori_loop(1, 32, send_e1, 0)
-
-    for plane in range(2):
-
+    def spread_p1(plane):
         def send_p1(d, carry):
             there, chip = near(d)
             rows = pl.ds(pl.multiple_of(16 * (2 * there + chip), 16), 16)
@@ -159,11 +150,29 @@
 
         lax.fori_loop(0, 16, send_p1, 0)
 
+    spread_p1(0)
+
+    def send_e1(d, carry):
+        i = (me + d) & 31
+        rows = pl.ds(pl.multiple_of(32 * i, 32), 32)
+        remote(e_snd.at[:, rows, :], e1.at[me], 1, (i >> 2, z, i & 3)).start()
+        return carry
+
+    lax.fori_loop(1, 32, send_e1, 0)
+
+    spread_p1(1)
+
     own_e = remote(eloc.at[mom], eloc.at[mom], 4, other_core)
     own_e.start()
     cross_e = remote(el_snd, eloc.at[mom], 7, other_chip)
     cross_e.start()
     e1[me] = e_snd[:, own_rows, :]
+
+    chunks = [pl.ds(pl.multiple_of(256 * e + 128 * i, 128), 128) for i in range(2)]
+    direct_p = []
+    for i in range(2):
+        part = pl_snd.at[:, pl.ds(128 * i, 128), :]
+        direct_p.append(remote(part, ploc.at[:, chunks[i], :], 17 + i, (src, z_loc, mom)))
 
     arrived(partbuf.at[pl.ds(0, 3)], 0)
     partners = [partbuf[o, 0, 0] for o in range(4)]
@@ -186,13 +195,7 @@
 
     spread_e2(0)
 
-    chunks = [pl.ds(pl.multiple_of(256 * e + 128 * i, 128), 128) for i in range(2)]
-    direct_p = []
-    for i in range(2):
-        part = pl_snd.at[:, pl.ds(128 * i, 128), :]
-        direct_p.append(remote(part, ploc.at[:, chunks[i], :], 17 + i, (src, z_loc, mom)))
-        direct_p[i].start()
-
+    spread_e2(1)
     for plane in range(2):
         arrived(p1[plane], 2 + plane)
 
@@ -206,8 +209,8 @@
 
         lax.fori_loop(1, 16, send_p2, 0)
         pmine[plane, :, own_strip, :] = p1[plane][(u + shift) & 15]
-    spread_e2(1)
-
+    direct_p[0].start()
+    direct_p[1].start()
     cross_e.wait_recv()
     from_chip = eloc.at[2 * (1 - c) + e]
     pass_e = remote(from_chip, from_chip, 10, other_core)

time: 64.2 us -> 59.8 us (0.931); the launches traced: 63.1 us -> 59.7 us
  Pallas kernels: 61.2 us -> 57.8 us
    pallas_call x1, Pallas kernels: 61.2 us -> 57.8 us  [shards(): pl.pallas_call(body, out_shape=jax.ShapeDtypeStruct((NSEP, 1, 2, 32), f32...]
where the time goes in v5:
time: 59.8 us; the launch traced here: 59.7 us
  Pallas kernels  57.8 us (97%)
  local copies, waits for them, and re-layouts  1.28 us (2%)
  between operations  0.66 us (1%)
    pallas_call x1, Pallas kernels, shards(): pl.pallas_call(body, out_shape=jax.ShapeDtypeStruct((NSEP, 1, 2, 32), f32...  57.8 us
    unnamed x1, local copies, waits for them, and re-layouts  1.28 us

profile of v5, /device:TPU:1, one launch (start us, length us, event | category | flops | bytes accessed | tf_op | source)
XLA Modules:
  0.0 59.7 jit_solution(12373897352652989641)
XLA Ops:
  0.7 57.8 %shard_map.64 = f32[4,1,2,32]{3,2,1,0:T(2,128)} custom-call(s32[4]{0:T(128)} %sep_hbm.1, s32[4,4]{1,0:T(4,128)} %gam_hbm.1, s32[1]{0:T(128)S(6)} %copy.8.part_hbm, s32[80]{0:T(128)} %constant.2.clone.tab_hbm, bf16[4,1,2,512,512]{4,3,2,1,0:T(8,128)(2,1)} %p_ref.1, bf16[4,1024,128]{2,1,0:T(8,128)(2,1)} %bitcast.2), custom_call_target="tpu_custom_call" | custom-call | tf_op jit(solution)/shard_map/pallas_call | solution.py:403
  58.4 1.3 %copy.9 = f32[32,4,1,2]{0,3,2,1:T(2,128)} copy(f32[32,4,1,2]{0,3,2,1:T(2,128)} %bitcast.3) | data formatting | bytes 2048

commit v6 on v4

v6 whole, which is shorter than its diff:
```python
import functools

import jax
import jax.numpy as jnp
import numpy as np
from jax import lax
from jax.experimental import pallas as pl
from jax.experimental.pallas import tpu as pltpu
from jax.sharding import PartitionSpec as P

MESH = pl.DeviceIdType.MESH
NSEP = 4


def gamma_table():
    unit = np.eye(4, dtype=complex)
    one = np.array([[0, 0, 0, 1j], [0, 0, 1j, 0], [0, -1j, 0, 0], [-1j, 0, 0, 0]])
    two = np.array([[0, 0, 0, -1], [0, 0, 1, 0], [0, 1, 0, 0], [-1, 0, 0, 0]], dtype=complex)
    three = np.array([[0, 0, 1j, 0], [0, 0, 0, -1j], [-1j, 0, 0, 0], [0, 1j, 0, 0]])
    four = np.array([[0, 0, 1, 0], [0, 0, 0, 1], [1, 0, 0, 0], [0, 1, 0, 0]], dtype=complex)
    rows = []
    for code in range(16):
        value = unit
        for position, factor in enumerate((one, two, three, four)):
            if code >> position & 1:
                value = value @ factor
        pattern = int(np.flatnonzero(np.abs(value[:, 0]))[0])
        powers = [(1, 1j, -1, -1j).index(complex(value[s ^ pattern, s])) for s in range(4)]
        rows.append([pattern] + powers)
    return np.array(rows, dtype=np.int32).reshape(-1)


def body(
    sep_hbm, gam_hbm, part_hbm, tab_hbm, p_ref, e_ref, out_ref,
    sep_ref, gam_ref, part_ref, tab_ref,
    e_in, p_in, e_snd, p_snd, pl_snd, el_snd, e1_0, e1_1, p1_re, p1_im, e2s, p2s, eloc, erem, ploc, pmine, pother,
    bacc, ptr, elt, erd, partbuf, res, r1, t2, r2, lsem, ssem, rsem,
):
    src, z, mom = lax.axis_index("src"), lax.axis_index("snk"), lax.axis_index("mom")
    c, e = mom >> 1, mom & 1
    u = 2 * src + c
    me = 4 * src + mom
    k = (z + 2) & 3
    z_even = 1 - (z & 1)
    z_rem = (z + 2 + 4 * z_even) & 7
    z_loc = (z + 6 + 4 * z_even) & 7
    p1 = (p1_re, p1_im)
    e1 = (e1_0, e1_1)

    def remote(src_ref, dst_ref, index, target):
        return pltpu.make_async_remote_copy(
            src_ref=src_ref, dst_ref=dst_ref, send_sem=ssem.at[index], recv_sem=rsem.at[index],
            device_id=target, device_id_type=MESH,
        )

    def arrived(ref, index):
        pltpu.make_async_copy(ref, ref, rsem.at[index]).wait()

    def left(ref, index):
        pltpu.make_async_copy(ref, ref, ssem.at[index]).wait()

    def near(d):
        flip = (d >> 2) & 1
        column = ((src >> 1) + d) & 3
        return 2 * column + ((src & 1) ^ flip), c ^ flip

    other_core = (src, z, 2 * c + 1 - e)
    other_chip = (src, z, 2 * (1 - c) + e)
    half = pl.ds(pl.multiple_of(256 * e, 256), 256)
    own_rows = [pl.ds(pl.multiple_of(32 * me + 16 * g, 16), 16) for g in range(2)]
    own_strip = pl.ds(pl.multiple_of(16 * u, 16), 16)

    loads = [
        pltpu.make_async_copy(one, two, lsem.at[index])
        for index, (one, two) in enumerate(
            (
                (part_hbm, part_ref),
                (sep_hbm, sep_ref),
                (gam_hbm, gam_ref),
                (tab_hbm, tab_ref),
                (e_ref, e_in),
                (p_ref.at[:, 0, :, half, :], p_in),
            )
        )
    ]
    for load in loads:
        load.start()

    barrier = pltpu.get_barrier_semaphore()

    def greet(target):
        pl.semaphore_signal(barrier, inc=1, device_id=target, device_id_type=MESH)

    def greet_blocks(d, carry):
        there, chip = near(d)
        greet((there, z_loc, 2 * chip + e))
        return carry

    def greet_plane(d, carry):
        i = (me + d) & 31
        greet((i >> 2, z, i & 3))
        return carry

    lax.fori_loop(0, 8, greet_blocks, 0)
    greet((src, z_rem, mom))
    for d in (1, 3, 4, 5, 7):
        greet((src, (z + d) & 7, mom))
    lax.fori_loop(1, 32, greet_plane, 0)

    for load in loads[:5]:
        load.wait()
    sep = sep_ref[k]
    odd = sep & 1
    is_a = ((z + (z >> 1) + (z >> 2)) & 1) == 1
    shift = jnp.where(is_a, sep >> 1, 16 - ((sep + 1) >> 1))
    par_loc = jnp.where(is_a, 0, (1 + odd) & 1)
    par_rem = jnp.where(is_a, odd, 1)
    time = (2 * u + jnp.where(is_a, 0, par_loc - sep)) & 31
    odd_own = sep_ref[z & 3] & 1
    snd_rem = jnp.where(z < NSEP, 1, odd_own)
    snd_loc = jnp.where(z < NSEP, 0, (1 + odd_own) & 1)
    partbuf[mom] = jnp.full((8, 128), part_ref[0], jnp.int32)
    for h in range(2):
        e_snd[h] = e_in[2 * h + par_rem]
    eloc[mom] = e_in[2 * c + par_loc]
    el_snd[...] = e_in[2 * (1 - c) + par_loc]
    loads[5].wait()
    for h in range(2):
        p_snd[:, h] = p_in[2 * h + snd_rem]
    for plane in range(2):
        pl_snd[:, pl.ds(512 * plane, 512)] = p_in[2 * c + snd_loc, plane]

    pl.semaphore_wait(barrier, 45)

    def send_partner(d, carry):
        remote(partbuf.at[mom], partbuf.at[mom], 0, (src, z, (mom + d) & 3)).start()
        return carry

    lax.fori_loop(1, 4, send_partner, 0)

    for g in range(2):

        def send_e1(d):
            i = (me + d) & 31
            rows = pl.ds(pl.multiple_of(32 * i + 16 * g, 16), 16)
            remote(e_snd.at[:, rows, :], e1[g].at[me], 1 + 18 * g, (i >> 2, z, i & 3)).start()

        def send_p1(d):
            there, chip = near(d)
            rows = pl.ds(pl.multiple_of(16 * (2 * there + chip), 16), 16)
            h = d >> 3
            remote(p_snd.at[g, h, rows, :], p1[g].at[2 * src + h], 2 + g, (there, z_rem, 2 * chip + e)).start()

        def send_both(d, carry):
            send_p1(d)
            send_e1(2 * d + 1)
            send_e1(2 * d + 2)
            return carry

        lax.fori_loop(0, 15, send_both, 0)
        send_p1(15)
        send_e1(31)
        e1[g][me] = e_snd[:, own_rows[g], :]

    own_e = remote(eloc.at[mom], eloc.at[mom], 4, other_core)
    own_e.start()
    cross_e = remote(el_snd, eloc.at[mom], 7, other_chip)
    cross_e.start()

    arrived(partbuf.at[pl.ds(0, 3)], 0)
    partners = [partbuf[o, 0, 0] for o in range(4)]

    def spread_p2(plane):
        arrived(p1[plane], 2 + plane)

        def send_p2(d, carry):
            j = (u + d) & 15
            p2s[plane, j] = p1[plane][(j + shift) & 15]
            remote(p2s.at[plane, j], pmine.at[plane, own_strip, :], 8 + plane, (j >> 1, z, 2 * (j & 1) + e)).start()
            return carry

        lax.fori_loop(1, 16, send_p2, 0)
        pmine[plane, own_strip, :] = p1[plane][(u + shift) & 15]

    def pick_e(g, i, a):
        block = ((i >> 1) + shift) & 15
        op = jnp.where(is_a, jnp.where((i & 1) == 0, partners[2 * a], partners[2 * a + 1]), (i & 1) + 2 * a)
        return e1[g][(block >> 1) * 4 + op, block & 1]

    def spread_e2(g):
        arrived(e1[g].at[pl.ds(0, 31)], 1 + 18 * g)

        def send_e2(d, carry):
            i = (me + d) & 31
            for a in range(2):
                e2s[g, i, a] = pick_e(g, i, a)
            remote(e2s.at[g, i], erem.at[:, own_rows[g], :], 5 + g, (i >> 2, z, i & 3)).start()
            return carry

        lax.fori_loop(1, 32, send_e2, 0)
        for a in range(2):
            erem[a, own_rows[g], :] = pick_e(g, me, a)

    spread_e2(0)
    spread_p2(0)
    spread_e2(1)
    spread_p2(1)

    chunks = [pl.ds(pl.multiple_of(256 * e + 128 * i, 128), 128) for i in range(2)]
    direct_p = []
    for i in range(2):
        part = pl_snd.at[pl.ds(128 * i, 128), :]
        direct_p.append(remote(part, ploc.at[chunks[i], :], 17 + i, (src, z_loc, mom)))
        direct_p[i].start()

    cross_e.wait_recv()
    from_chip = eloc.at[2 * (1 - c) + e]
    pass_e = remote(from_chip, from_chip, 10, other_core)
    pass_e.start()
    pass_p, pass_r = [], []

    def pass_local(i):
        direct_p[i].wait_recv()
        part = ploc.at[chunks[i], :]
        pass_p.append(remote(part, part, 11 + i, other_core))
        pass_p[i].start()

    own_e.wait_recv()
    pass_e.wait_recv()

    def loc_op(a):
        return jnp.where(is_a, e + 2 * a, partbuf[e + 2 * a, 0, 0])

    def turn(step, carry):
        rows = pl.ds(pl.multiple_of(128 * (step & 7), 128), 128)
        ptr[step] = eloc[loc_op(step >> 3), rows, :].astype(jnp.float32).T
        return carry

    lax.fori_loop(0, 16, turn, 0)

    def phased(op, s, take):
        sum_re = [jnp.zeros((128, 128), jnp.float32) for _ in range(4)]
        sum_im = [jnp.zeros((128, 128), jnp.float32) for _ in range(4)]
        for r in range(4):
            code = gam_ref[op, r]
            pattern = tab_ref[5 * code]
            power = tab_ref[5 * code + 1 + s]
            ca = jnp.where(power == 0, 1.0, jnp.where(power == 2, -1.0, 0.0))
            cb = jnp.where(power == 1, 1.0, jnp.where(power == 3, -1.0, 0.0))
            t_re, t_im = take(r)
            v_re = ca * t_re - cb * t_im
            v_im = ca * t_im + cb * t_re
            for s_left in range(4):
                here = jnp.where((s ^ pattern) == s_left, 1.0, 0.0)
                sum_re[s_left] += here * v_re
                sum_im[s_left] += here * v_im
        return sum_re, sum_im

    def build(step, carry):
        a, s = step >> 2, step & 3
        sum_re, sum_im = phased(loc_op(a), s, lambda r: (ptr[8 * a + 2 * r], ptr[8 * a + 2 * r + 1]))
        rows = pl.ds(pl.multiple_of(128 * s, 128), 128)
        more = pl.ds(pl.multiple_of(512 + 128 * s, 128), 128)
        for s_left in range(4):
            real, imag = sum_re[s_left].astype(jnp.bfloat16), sum_im[s_left].astype(jnp.bfloat16)
            elt[a, rows, pl.ds(128 * s_left, 128)] = real
            elt[a, rows, pl.ds(512 + 128 * s_left, 128)] = -imag
            elt[a, more, pl.ds(128 * s_left, 128)] = imag
            elt[a, more, pl.ds(512 + 128 * s_left, 128)] = real
        return carry

    lax.fori_loop(0, 8, build, 0)

    def pass_remote(plane):
        arrived(p1[plane].at[pl.ds(0, 15)], 8 + plane)
        pass_r.append(remote(pmine.at[plane], pother.at[plane], 13 + plane, other_core))
        pass_r[plane].start()

    pass_remote(0)

    for g in range(2):
        arrived(e1[g].at[pl.ds(0, 31)], 5 + g)

    def build_remote(step, carry):
        a, s = step >> 2, step & 3
        op = jnp.where(is_a, partbuf[e + 2 * a, 0, 0], e + 2 * a)

        def take(r):
            return (
                erem[a, pl.ds(256 * r, 128), :].astype(jnp.float32),
                erem[a, pl.ds(256 * r + 128, 128), :].astype(jnp.float32),
            )

        sum_re, sum_im = phased(op, s, take)
        first = pl.ds(pl.multiple_of(128 * s, 128), 128)
        second = pl.ds(pl.multiple_of(512 + 128 * s, 128), 128)
        for s_left in range(4):
            rows = pl.ds(128 * s_left, 128)
            real, imag = sum_re[s_left].astype(jnp.bfloat16), sum_im[s_left].astype(jnp.bfloat16)
            erd[a, 0, rows, first] = real
            erd[a, 0, rows, second] = imag
            erd[a, 1, rows, first] = -imag
            erd[a, 1, rows, second] = real
        return carry

    lax.fori_loop(0, 8, build_remote, 0)

    def times_elemental(block, which, plane):
        rows = pl.ds(pl.multiple_of(256 * which, 256), 256)

        def product(step, carry):
            cols = pl.ds(pl.multiple_of(256 * step, 256), 256)
            for a in range(2):
                part = jnp.dot(block[plane], erd[a, plane, :, cols], preferred_element_type=jnp.float32)
                if plane == 0:
                    bacc[a, rows, cols] = part
                else:
                    bacc[a, rows, cols] += part
            return carry

        lax.fori_loop(0, 4, product, 0)

    def close(i, totals):
        right = jnp.concatenate([ploc[pl.ds(128 * i, 128), :], ploc[pl.ds(256 + 128 * i, 128), :]], axis=0)
        new = []
        for a in range(2):
            g = lax.dot_general(elt[a], right, (((1,), (1,)), ((), ())), preferred_element_type=jnp.float32)
            acc_re, acc_im = totals[a]
            for part in range(2):
                g_re, g_im = g[:512, 128 * part : 128 * part + 128], g[512:, 128 * part : 128 * part + 128]
                b_re = bacc[a, :, pl.ds(256 * part + 128 * i, 128)]
                b_im = bacc[a, :, pl.ds(512 + 256 * part + 128 * i, 128)]
                acc_re += jnp.sum((b_re * g_re - b_im * g_im).reshape(64, 8, 128), axis=0)
                acc_im += jnp.sum((b_re * g_im + b_im * g_re).reshape(64, 8, 128), axis=0)
            new.append((acc_re, acc_im))
        return new

    times_elemental(pmine, e, 0)
    pass_r[0].wait_recv()
    times_elemental(pother, 1 - e, 0)
    pass_remote(1)
    times_elemental(pmine, e, 1)
    pass_local(0)
    pass_r[1].wait_recv()
    times_elemental(pother, 1 - e, 1)
    zero = jnp.zeros((8, 128), jnp.float32)
    totals = [(zero, zero), (zero, zero)]
    pass_p[0].wait_recv()
    pass_local(1)
    totals = close(0, totals)
    pass_p[1].wait_recv()
    totals = close(1, totals)
    lane = lax.broadcasted_iota(jnp.int32, (8, 128), 1)
    row = lax.broadcasted_iota(jnp.int32, (8, 128), 0)
    tile = jnp.zeros((8, 128), jnp.float32)
    for a in range(2):
        for part in range(2):
            here = (lane == time + 32 * a) & (row == 2 * k + part)
            tile += jnp.where(here, jnp.sum(totals[a][part]) / 512, 0.0)
    res[...] = tile

    def send_r1(d, carry):
        remote(res, r1.at[z], 15, (src, (z + d) & 7, mom)).start()
        return carry

    lax.fori_loop(1, 8, send_r1, 0)
    r1[z] = res[...]
    arrived(r1.at[pl.ds(0, 7)], 15)
    t2[...] = jnp.sum(r1[...], axis=0)

    def send_r2(d, carry):
        j = (u + d) & 15
        remote(t2, r2.at[u], 16, (j >> 1, z, 2 * (j & 1) + e)).start()
        return carry

    lax.fori_loop(1, 16, send_r2, 0)
    r2[u] = t2[...]
    arrived(r2.at[pl.ds(0, 15)], 16)
    total = jnp.sum(r2[...], axis=0)
    for kk in range(NSEP):
        two = total[2 * kk : 2 * kk + 2]
        out_ref[kk, 0] = jnp.where(c == 0, two[:, :32], two[:, 32:64])

    left(partbuf.at[pl.ds(0, 3)], 0)
    for g in range(2):
        left(e1[g].at[pl.ds(0, 31)], 1 + 18 * g)
        left(e1[g].at[pl.ds(0, 31)], 5 + g)
    for plane in range(2):
        left(p1[plane], 2 + plane)
        left(p1[plane].at[pl.ds(0, 15)], 8 + plane)
    for copy in [own_e, cross_e, pass_e] + direct_p + pass_p + pass_r:
        copy.wait_send()
    left(r1.at[pl.ds(0, 7)], 15)
    left(r2.at[pl.ds(0, 15)], 16)


def shards(peram_blocks, projections, gamma_index, partner, separations):
    bf, f32, i32 = jnp.bfloat16, jnp.float32, jnp.int32
    buffers = [
        ((4, 1024, 128), bf),
        ((4, 2, 256, 512), bf),
        ((2, 1024, 128), bf),
        ((2, 2, 256, 512), bf),
        ((256, 1024), bf),
        ((1024, 128), bf),
        ((32, 2, 16, 128), bf),
        ((32, 2, 16, 128), bf),
        ((16, 16, 512), bf),
        ((16, 16, 512), bf),
        ((2, 32, 2, 16, 128), bf),
        ((2, 16, 16, 512), bf),
        ((4, 1024, 128), bf),
        ((2, 1024, 128), bf),
        ((512, 1024), bf),
        ((2, 256, 512), bf),
        ((2, 256, 512), bf),
        ((2, 512, 1024), f32),
        ((16, 128, 128), f32),
        ((2, 1024, 1024), bf),
        ((2, 2, 512, 1024), bf),
        ((4, 8, 128), i32),
        ((8, 128), f32),
        ((8, 8, 128), f32),
        ((8, 128), f32),
        ((16, 8, 128), f32),
    ]
    out = pl.pallas_call(
        body,
        out_shape=jax.ShapeDtypeStruct((NSEP, 1, 2, 32), f32),
        in_specs=[pl.BlockSpec(memory_space=pltpu.HBM)] * 6,
        out_specs=pl.BlockSpec(memory_space=pltpu.VMEM),
        scratch_shapes=[pltpu.SMEM(shape, i32) for shape in ((4,), (4, 4), (1,), (80,))]
        + [pltpu.VMEM(shape, dtype) for shape, dtype in buffers]
        + [pltpu.SemaphoreType.DMA((count,)) for count in (6, 20, 20)],
        compiler_params=pltpu.CompilerParams(
            collective_id=0, has_side_effects=True, vmem_limit_bytes=64 * 1024 * 1024 - 65536
        ),
    )(
        separations,
        gamma_index,
        partner,
        jnp.asarray(gamma_table()),
        peram_blocks,
        projections.reshape(4, 1024, 128),
    )
    return jnp.transpose(out, (3, 0, 1, 2))


def solution(mesh):
    placed = (
        P("src", "snk", None, None, None),
        P("src", "mom", None, None, None, None),
        P(),
        P("mom"),
        P(),
    )
    return jax.shard_map(
        shards, mesh=mesh, in_specs=placed, out_specs=P(None, None, "mom", None), check_vma=False
    )
```

time: 64.2 us -> 58.7 us (0.914); the launches traced: 63.1 us -> 58.5 us
  Pallas kernels: 61.2 us -> 56.6 us
    pallas_call x1, Pallas kernels: 61.2 us -> 56.6 us  [shards(): pl.pallas_call(body, out_shape=jax.ShapeDtypeStruct((NSEP, 1, 2, 32), f32...]
where the time goes in v6:
time: 58.7 us; the launch traced here: 58.5 us
  Pallas kernels  56.6 us (96%)
  local copies, waits for them, and re-layouts  1.28 us (2%)
  between operations  0.66 us (1%)
    pallas_call x1, Pallas kernels, shards(): pl.pallas_call(body, out_shape=jax.ShapeDtypeStruct((NSEP, 1, 2, 32), f32...  56.6 us
    unnamed x1, local copies, waits for them, and re-layouts  1.28 us

profile of v6, /device:TPU:1, one launch (start us, length us, event | category | flops | bytes accessed | tf_op | source)
XLA Modules:
  0.0 58.5 jit_solution(8920793077690835468)
XLA Ops:
  0.7 56.6 %shard_map.64 = f32[4,1,2,32]{3,2,1,0:T(2,128)} custom-call(s32[4]{0:T(128)} %sep_hbm.1, s32[4,4]{1,0:T(4,128)} %gam_hbm.1, s32[1]{0:T(128)S(6)} %copy.8.part_hbm, s32[80]{0:T(128)} %constant.2.clone.tab_hbm, bf16[4,1,2,512,512]{4,3,2,1,0:T(8,128)(2,1)} %p_ref.1, bf16[4,1024,128]{2,1,0:T(8,128)(2,1)} %bitcast.2), custom_call_target="tpu_custom_call" | custom-call | tf_op jit(solution)/shard_map/pallas_call | solution.py:427
  57.3 1.3 %copy.9 = f32[32,4,1,2]{0,3,2,1:T(2,128)} copy(f32[32,4,1,2]{0,3,2,1:T(2,128)} %bitcast.3) | data formatting | bytes 2048

commit v7 on v6

--- a/solution.py
+++ b/solution.py
@@ -34,7 +34,7 @@
     sep_hbm, gam_hbm, part_hbm, tab_hbm, p_ref, e_ref, out_ref,
     sep_ref, gam_ref, part_ref, tab_ref,
     e_in, p_in, e_snd, p_snd, pl_snd, el_snd, e1_0, e1_1, p1_re, p1_im, e2s, p2s, eloc, erem, ploc, pmine, pother,
-    bacc, ptr, elt, erd, partbuf, res, r1, t2, r2, lsem, ssem, rsem,
+    bacc, tabl, tabr, elt, erd, partbuf, res, r1, t2, r2, lsem, ssem, rsem,
 ):
     src, z, mom = lax.axis_index("src"), lax.axis_index("snk"), lax.axis_index("mom")
     c, e = mom >> 1, mom & 1
@@ -130,6 +130,11 @@
     for plane in range(2):
         pl_snd[:, pl.ds(512 * plane, 512)] = p_in[2 * c + snd_loc, plane]
 
+    for a in range(2):
+        for r in range(4):
+            tabl[a, r, 4] = jnp.zeros((128, 128), jnp.float32)
+            tabr[a, r, 4] = jnp.zeros((128, 128), jnp.float32)
+
     pl.semaphore_wait(barrier, 45)
 
     def send_partner(d, carry):
@@ -231,38 +236,35 @@
     def loc_op(a):
         return jnp.where(is_a, e + 2 * a, partbuf[e + 2 * a, 0, 0])
 
+    def fill(table, step, value):
+        a, r, plane = step >> 3, (step >> 1) & 3, step & 1
+        table[a, r, plane] = value
+        table[a, r, 2 + plane] = -value
+
     def turn(step, carry):
         rows = pl.ds(pl.multiple_of(128 * (step & 7), 128), 128)
-        ptr[step] = eloc[loc_op(step >> 3), rows, :].astype(jnp.float32).T
+        fill(tabl, step, eloc[loc_op(step >> 3), rows, :].astype(jnp.float32).T)
         return carry
 
     lax.fori_loop(0, 16, turn, 0)
 
-    def phased(op, s, take):
-        sum_re = [jnp.zeros((128, 128), jnp.float32) for _ in range(4)]
-        sum_im = [jnp.zeros((128, 128), jnp.float32) for _ in range(4)]
+    def phased(table, a, op, s, s_left):
+        parts = [None, None]
         for r in range(4):
             code = gam_ref[op, r]
-            pattern = tab_ref[5 * code]
             power = tab_ref[5 * code + 1 + s]
-            ca = jnp.where(power == 0, 1.0, jnp.where(power == 2, -1.0, 0.0))
-            cb = jnp.where(power == 1, 1.0, jnp.where(power == 3, -1.0, 0.0))
-            t_re, t_im = take(r)
-            v_re = ca * t_re - cb * t_im
-            v_im = ca * t_im + cb * t_re
-            for s_left in range(4):
-                here = jnp.where((s ^ pattern) == s_left, 1.0, 0.0)
-                sum_re[s_left] += here * v_re
-                sum_im[s_left] += here * v_im
-        return sum_re, sum_im
+            hit = (s ^ tab_ref[5 * code]) == s_left
+            for part in range(2):
+                term = table[a, r, jnp.where(hit, (4 + part - power) & 3, 4)]
+                parts[part] = term if r == 0 else parts[part] + term
+        return parts[0].astype(jnp.bfloat16), parts[1].astype(jnp.bfloat16)
 
     def build(step, carry):
         a, s = step >> 2, step & 3
-        sum_re, sum_im = phased(loc_op(a), s, lambda r: (ptr[8 * a + 2 * r], ptr[8 * a + 2 * r + 1]))
         rows = pl.ds(pl.multiple_of(128 * s, 128), 128)
         more = pl.ds(pl.multiple_of(512 + 128 * s, 128), 128)
         for s_left in range(4):
-            real, imag = sum_re[s_left].astype(jnp.bfloat16), sum_im[s_left].astype(jnp.bfloat16)
+            real, imag = phased(tabl, a, loc_op(a), s, s_left)
             elt[a, rows, pl.ds(128 * s_left, 128)] = real
             elt[a, rows, pl.ds(512 + 128 * s_left, 128)] = -imag
             elt[a, more, pl.ds(128 * s_left, 128)] = imag
@@ -285,24 +287,23 @@
         a, s = step >> 2, step & 3
         op = jnp.where(is_a, partbuf[e + 2 * a, 0, 0], e + 2 * a)
 
-        def take(r):
-            return (
-                erem[a, pl.ds(256 * r, 128), :].astype(jnp.float32),
-                erem[a, pl.ds(256 * r + 128, 128), :].astype(jnp.float32),
-            )
-
-        sum_re, sum_im = phased(op, s, take)
         first = pl.ds(pl.multiple_of(128 * s, 128), 128)
         second = pl.ds(pl.multiple_of(512 + 128 * s, 128), 128)
         for s_left in range(4):
             rows = pl.ds(128 * s_left, 128)
-            real, imag = sum_re[s_left].astype(jnp.bfloat16), sum_im[s_left].astype(jnp.bfloat16)
+            real, imag = phased(tabr, a, op, s, s_left)
             erd[a, 0, rows, first] = real
             erd[a, 0, rows, second] = imag
             erd[a, 1, rows, first] = -imag
             erd[a, 1, rows, second] = real
         return carry
 
+    def take(step, carry):
+        rows = pl.ds(pl.multiple_of(128 * (step & 7), 128), 128)
+        fill(tabr, step, erem[step >> 3, rows, :].astype(jnp.float32))
+        return carry
+
+    lax.fori_loop(0, 16, take, 0)
     lax.fori_loop(0, 8, build_remote, 0)
 
     def times_elemental(block, which, plane):
@@ -415,7 +416,8 @@
         ((2, 256, 512), bf),
         ((2, 256, 512), bf),
         ((2, 512, 1024), f32),
-        ((16, 128, 128), f32),
+        ((2, 4, 5, 128, 128), f32),
+        ((2, 4, 5, 128, 128), f32),
         ((2, 1024, 1024), bf),
         ((2, 2, 512, 1024), bf),
         ((4, 8, 128), i32),

time: 58.7 us -> 57.6 us (0.981)
  Pallas kernels: 56.6 us -> 55.6 us
    pallas_call x1, Pallas kernels: 56.6 us -> 55.6 us  [shards(): pl.pallas_call(body, out_shape=jax.ShapeDtypeStruct((NSEP, 1, 2, 32), f32...]
where the time goes in v7:
time: 57.6 us; the launch traced here: 57.5 us
  Pallas kernels  55.6 us (97%)
  local copies, waits for them, and re-layouts  1.28 us (2%)
  between operations  0.66 us (1%)
    pallas_call x1, Pallas kernels, shards(): pl.pallas_call(body, out_shape=jax.ShapeDtypeStruct((NSEP, 1, 2, 32), f32...  55.6 us
    unnamed x1, local copies, waits for them, and re-layouts  1.28 us

profile of v7, /device:TPU:1, one launch (start us, length us, event | category | flops | bytes accessed | tf_op | source)
XLA Modules:
  0.0 57.5 jit_solution(5403138161626433534)
XLA Ops:
  0.7 55.6 %shard_map.64 = f32[4,1,2,32]{3,2,1,0:T(2,128)} custom-call(s32[4]{0:T(128)} %sep_hbm.1, s32[4,4]{1,0:T(4,128)} %gam_hbm.1, s32[1]{0:T(128)S(6)} %copy.8.part_hbm, s32[80]{0:T(128)} %constant.2.clone.tab_hbm, bf16[4,1,2,512,512]{4,3,2,1,0:T(8,128)(2,1)} %p_ref.1, bf16[4,1024,128]{2,1,0:T(8,128)(2,1)} %bitcast.2), custom_call_target="tpu_custom_call" | custom-call | tf_op jit(solution)/shard_map/pallas_call | solution.py:429
  56.2 1.3 %copy.9 = f32[32,4,1,2]{0,3,2,1:T(2,128)} copy(f32[32,4,1,2]{0,3,2,1:T(2,128)} %bitcast.3) | data formatting | bytes 2048

commit v8 on v7

--- a/solution.py
+++ b/solution.py
@@ -33,7 +33,7 @@
 def body(
     sep_hbm, gam_hbm, part_hbm, tab_hbm, p_ref, e_ref, out_ref,
     sep_ref, gam_ref, part_ref, tab_ref,
-    e_in, p_in, e_snd, p_snd, pl_snd, el_snd, e1_0, e1_1, p1_re, p1_im, e2s, p2s, eloc, erem, ploc, pmine, pother,
+    e_in, p_in, e_snd, p_snd, pl_snd, el_snd, e1_0, e1_1, p1_re, p1_im, e2s, p2s, eloc, erem, ploc, prem,
     bacc, tabl, tabr, elt, erd, partbuf, res, r1, t2, r2, lsem, ssem, rsem,
 ):
     src, z, mom = lax.axis_index("src"), lax.axis_index("snk"), lax.axis_index("mom")
@@ -68,7 +68,7 @@
     other_chip = (src, z, 2 * (1 - c) + e)
     half = pl.ds(pl.multiple_of(256 * e, 256), 256)
     own_rows = [pl.ds(pl.multiple_of(32 * me + 16 * g, 16), 16) for g in range(2)]
-    own_strip = pl.ds(pl.multiple_of(16 * u, 16), 16)
+    own_strip = pl.ds(pl.multiple_of(256 * e + 16 * u, 16), 16)
 
     loads = [
         pltpu.make_async_copy(one, two, lsem.at[index])
@@ -83,9 +83,6 @@
             )
         )
     ]
-    for load in loads:
-        load.start()
-
     barrier = pltpu.get_barrier_semaphore()
 
     def greet(target):
@@ -105,6 +102,8 @@
     greet((src, z_rem, mom))
     for d in (1, 3, 4, 5, 7):
         greet((src, (z + d) & 7, mom))
+    for load in loads:
+        load.start()
     lax.fori_loop(1, 32, greet_plane, 0)
 
     for load in loads[:5]:
@@ -146,7 +145,7 @@
     for g in range(2):
 
         def send_e1(d):
-            i = (me + d) & 31
+            i = (me + 13 * d) & 31
             rows = pl.ds(pl.multiple_of(32 * i + 16 * g, 16), 16)
             remote(e_snd.at[:, rows, :], e1[g].at[me], 1 + 18 * g, (i >> 2, z, i & 3)).start()
 
@@ -179,13 +178,13 @@
         arrived(p1[plane], 2 + plane)
 
         def send_p2(d, carry):
-            j = (u + d) & 15
+            j = (u + 5 * d) & 15
             p2s[plane, j] = p1[plane][(j + shift) & 15]
-            remote(p2s.at[plane, j], pmine.at[plane, own_strip, :], 8 + plane, (j >> 1, z, 2 * (j & 1) + e)).start()
+            remote(p2s.at[plane, j], prem.at[plane, own_strip, :], 8 + plane, (j >> 1, z, 2 * (j & 1) + e)).start()
             return carry
 
         lax.fori_loop(1, 16, send_p2, 0)
-        pmine[plane, own_strip, :] = p1[plane][(u + shift) & 15]
+        prem[plane, own_strip, :] = p1[plane][(u + shift) & 15]
 
     def pick_e(g, i, a):
         block = ((i >> 1) + shift) & 15
@@ -196,7 +195,7 @@
         arrived(e1[g].at[pl.ds(0, 31)], 1 + 18 * g)
 
         def send_e2(d, carry):
-            i = (me + d) & 31
+            i = (me + 13 * d) & 31
             for a in range(2):
                 e2s[g, i, a] = pick_e(g, i, a)
             remote(e2s.at[g, i], erem.at[:, own_rows[g], :], 5 + g, (i >> 2, z, i & 3)).start()
@@ -275,7 +274,8 @@
 
     def pass_remote(plane):
         arrived(p1[plane].at[pl.ds(0, 15)], 8 + plane)
-        pass_r.append(remote(pmine.at[plane], pother.at[plane], 13 + plane, other_core))
+        own_half = prem.at[plane, half, :]
+        pass_r.append(remote(own_half, own_half, 13 + plane, other_core))
         pass_r[plane].start()
 
     pass_remote(0)
@@ -306,20 +306,13 @@
     lax.fori_loop(0, 16, take, 0)
     lax.fori_loop(0, 8, build_remote, 0)
 
-    def times_elemental(block, which, plane):
-        rows = pl.ds(pl.multiple_of(256 * which, 256), 256)
-
-        def product(step, carry):
-            cols = pl.ds(pl.multiple_of(256 * step, 256), 256)
-            for a in range(2):
-                part = jnp.dot(block[plane], erd[a, plane, :, cols], preferred_element_type=jnp.float32)
-                if plane == 0:
-                    bacc[a, rows, cols] = part
-                else:
-                    bacc[a, rows, cols] += part
-            return carry
-
-        lax.fori_loop(0, 4, product, 0)
+    def times_elemental(plane):
+        for a in range(2):
+            part = jnp.dot(prem[plane], erd[a, plane], preferred_element_type=jnp.float32)
+            if plane == 0:
+                bacc[a] = part
+            else:
+                bacc[a] += part
 
     def close(i, totals):
         right = jnp.concatenate([ploc[pl.ds(128 * i, 128), :], ploc[pl.ds(256 + 128 * i, 128), :]], axis=0)
@@ -336,14 +329,12 @@
             new.append((acc_re, acc_im))
         return new
 
-    times_elemental(pmine, e, 0)
     pass_r[0].wait_recv()
-    times_elemental(pother, 1 - e, 0)
+    times_elemental(0)
     pass_remote(1)
-    times_elemental(pmine, e, 1)
     pass_local(0)
     pass_r[1].wait_recv()
-    times_elemental(pother, 1 - e, 1)
+    times_elemental(1)
     zero = jnp.zeros((8, 128), jnp.float32)
     totals = [(zero, zero), (zero, zero)]
     pass_p[0].wait_recv()
@@ -357,7 +348,8 @@
     for a in range(2):
         for part in range(2):
             here = (lane == time + 32 * a) & (row == 2 * k + part)
-            tile += jnp.where(here, jnp.sum(totals[a][part]) / 512, 0.0)
+            value = jnp.sum(jnp.sum(totals[a][part], axis=0, keepdims=True), axis=1, keepdims=True)
+            tile += jnp.where(here, value * (1.0 / 512), 0.0)
     res[...] = tile
 
     def send_r1(d, carry):
@@ -413,8 +405,7 @@
         ((4, 1024, 128), bf),
         ((2, 1024, 128), bf),
         ((512, 1024), bf),
-        ((2, 256, 512), bf),
-        ((2, 256, 512), bf),
+        ((2, 512, 512), bf),
         ((2, 512, 1024), f32),
         ((2, 4, 5, 128, 128), f32),
         ((2, 4, 5, 128, 128), f32),

time: 57.6 us -> 56.2 us (0.976)
  Pallas kernels: 55.6 us -> 54.1 us
    pallas_call x1, Pallas kernels: 55.6 us -> 54.1 us  [shards(): pl.pallas_call(body, out_shape=jax.ShapeDtypeStruct((NSEP, 1, 2, 32), f32...]
where the time goes in v8:
time: 56.2 us; the launch traced here: 56.1 us
  Pallas kernels  54.1 us (96%)
  local copies, waits for them, and re-layouts  1.28 us (2%)
  between operations  0.66 us (1%)
    pallas_call x1, Pallas kernels, shards(): pl.pallas_call(body, out_shape=jax.ShapeDtypeStruct((NSEP, 1, 2, 32), f32...  54.1 us
    unnamed x1, local copies, waits for them, and re-layouts  1.28 us

profile of v8, /device:TPU:1, one launch (start us, length us, event | category | flops | bytes accessed | tf_op | source)
XLA Modules:
  0.0 56.1 jit_solution(2882668678122786561)
XLA Ops:
  0.7 54.1 %shard_map.64 = f32[4,1,2,32]{3,2,1,0:T(2,128)} custom-call(s32[4]{0:T(128)} %sep_hbm.1, s32[4,4]{1,0:T(4,128)} %gam_hbm.1, s32[1]{0:T(128)S(6)} %copy.8.part_hbm, s32[80]{0:T(128)} %constant.2.clone.tab_hbm, bf16[4,1,2,512,512]{4,3,2,1,0:T(8,128)(2,1)} %p_ref.1, bf16[4,1024,128]{2,1,0:T(8,128)(2,1)} %bitcast.2), custom_call_target="tpu_custom_call" | custom-call | tf_op jit(solution)/shard_map/pallas_call | solution.py:420
  54.8 1.3 %copy.9 = f32[32,4,1,2]{0,3,2,1:T(2,128)} copy(f32[32,4,1,2]{0,3,2,1:T(2,128)} %bitcast.3) | data formatting | bytes 2048

commit v9 on v8

--- a/solution.py
+++ b/solution.py
@@ -210,11 +210,12 @@
     spread_e2(1)
     spread_p2(1)
 
-    chunks = [pl.ds(pl.multiple_of(256 * e + 128 * i, 128), 128) for i in range(2)]
+    spans = ((0, 128), (128, 64), (192, 64))
+    chunks = [pl.ds(pl.multiple_of(256 * e + first, 64), count) for first, count in spans]
     direct_p = []
-    for i in range(2):
-        part = pl_snd.at[pl.ds(128 * i, 128), :]
-        direct_p.append(remote(part, ploc.at[chunks[i], :], 17 + i, (src, z_loc, mom)))
+    for i, (first, count) in enumerate(spans):
+        part = pl_snd.at[pl.ds(first, count), :]
+        direct_p.append(remote(part, ploc.at[chunks[i], :], (17, 18, 20)[i], (src, z_loc, mom)))
         direct_p[i].start()
 
     cross_e.wait_recv()
@@ -226,7 +227,7 @@
     def pass_local(i):
         direct_p[i].wait_recv()
         part = ploc.at[chunks[i], :]
-        pass_p.append(remote(part, part, 11 + i, other_core))
+        pass_p.append(remote(part, part, (11, 12, 21)[i], other_core))
         pass_p[i].start()
 
     own_e.wait_recv()
@@ -339,8 +340,10 @@
     totals = [(zero, zero), (zero, zero)]
     pass_p[0].wait_recv()
     pass_local(1)
+    pass_local(2)
     totals = close(0, totals)
     pass_p[1].wait_recv()
+    pass_p[2].wait_recv()
     totals = close(1, totals)
     lane = lax.broadcasted_iota(jnp.int32, (8, 128), 1)
     row = lax.broadcasted_iota(jnp.int32, (8, 128), 0)
@@ -424,7 +427,7 @@
         out_specs=pl.BlockSpec(memory_space=pltpu.VMEM),
         scratch_shapes=[pltpu.SMEM(shape, i32) for shape in ((4,), (4, 4), (1,), (80,))]
         + [pltpu.VMEM(shape, dtype) for shape, dtype in buffers]
-        + [pltpu.SemaphoreType.DMA((count,)) for count in (6, 20, 20)],
+        + [pltpu.SemaphoreType.DMA((count,)) for count in (6, 22, 22)],
         compiler_params=pltpu.CompilerParams(
             collective_id=0, has_side_effects=True, vmem_limit_bytes=64 * 1024 * 1024 - 65536
         ),

time: 56.2 us -> 56.2 us (level)
  no operation moved by 1% of the time
where the time goes in v9:
time: 56.2 us; the launch traced here: 56.1 us
  Pallas kernels  54.1 us (96%)
  local copies, waits for them, and re-layouts  1.28 us (2%)
  between operations  0.66 us (1%)
    pallas_call x1, Pallas kernels, shards(): pl.pallas_call(body, out_shape=jax.ShapeDtypeStruct((NSEP, 1, 2, 32), f32...  54.1 us
    unnamed x1, local copies, waits for them, and re-layouts  1.28 us

profile of v9, /device:TPU:1, one launch (start us, length us, event | category | flops | bytes accessed | tf_op | source)
XLA Modules:
  0.0 56.1 jit_solution(9174113623258182486)
XLA Ops:
  0.7 54.1 %shard_map.64 = f32[4,1,2,32]{3,2,1,0:T(2,128)} custom-call(s32[4]{0:T(128)} %sep_hbm.1, s32[4,4]{1,0:T(4,128)} %gam_hbm.1, s32[1]{0:T(128)S(6)} %copy.8.part_hbm, s32[80]{0:T(128)} %constant.2.clone.tab_hbm, bf16[4,1,2,512,512]{4,3,2,1,0:T(8,128)(2,1)} %p_ref.1, bf16[4,1024,128]{2,1,0:T(8,128)(2,1)} %bitcast.2), custom_call_target="tpu_custom_call" | custom-call | tf_op jit(solution)/shard_map/pallas_call | solution.py:423
  54.8 1.3 %copy.9 = f32[32,4,1,2]{0,3,2,1:T(2,128)} copy(f32[32,4,1,2]{0,3,2,1:T(2,128)} %bitcast.3) | data formatting | bytes 2048
